TPU v7x, 512 devices: a whole 4x4x16 slice. The times are simulated.
512 devices in a mesh: dp: 32 (over x, y, core), tensor: 16 (over z).
Axes of the slice: x: 4, y: 4, z: 16, core: 2. Of those that a mesh axis runs over, the one named last changes fastest.
Arguments:
- grad: bfloat16 [32, 2048, 4096], P('dp', 'tensor'), may hold values from -6 to 6
- error: bfloat16 [32, 2048, 4096], P('dp', 'tensor'), may hold values from -4 to 4
- q_start: bfloat16 [4096, 64], P('tensor'), may hold values from -6 to 6
Outputs:
- update: bfloat16 [2048, 4096], P('tensor')
- new_error: bfloat16 [32, 2048, 4096], P('dp', 'tensor')
- q_new: float32 [4096, 64], P('tensor')
All inputs are finite; a program needn't handle non-finite values.
Results may differ from a plain program's by a relative error of at most 0.012.
Values may be sent and summed in bfloat16 or wider, within the bound.
No kernel may reach another device: no remote copies, remote signals or barrier semaphores. Data moves between devices by JAX's collectives and lax.ppermute only.
A program may use at most 64 MiB of HBM per device.

v0:
```python
import jax
import jax.numpy as jnp
from jax import lax
from jax.sharding import PartitionSpec as P

D = 4096


def body(grad, error, q_start):
    corrected = (grad[0].astype(jnp.float32) + error[0].astype(jnp.float32)).astype(jnp.bfloat16)
    replicas = lax.axis_size("dp")
    local_p = jnp.dot(
        corrected,
        lax.all_gather(q_start, "tensor", axis=0, tiled=True),
        preferred_element_type=jnp.float32,
    )
    p_sum = lax.psum(local_p, "dp")
    gram = lax.psum(jnp.dot(p_sum.T, p_sum, precision=lax.Precision.HIGHEST), "tensor")
    lower = lax.linalg.cholesky(gram)
    p_hat = lax.linalg.triangular_solve(lower, p_sum, left_side=False, lower=True, transpose_a=True)
    p_round = p_hat.astype(jnp.bfloat16)
    block_rows = D // lax.axis_size("tensor")
    term = lax.dot_general(
        corrected, p_round, (((0,), (0,)), ((), ())), preferred_element_type=jnp.float32
    )
    q_full = lax.psum(term, ("dp", "tensor")) / replicas
    q_round = q_full.astype(jnp.bfloat16)
    q_mine = lax.dynamic_slice_in_dim(q_full, lax.axis_index("tensor") * block_rows, block_rows, 0)
    full_update = lax.dot_general(
        p_round, q_round, (((1,), (1,)), ((), ())), preferred_element_type=jnp.float32
    )
    new_error = (corrected.astype(jnp.float32) - full_update).astype(jnp.bfloat16)[None]
    return (full_update.astype(jnp.bfloat16), new_error, q_mine)


def solution(mesh):
    placed = (P("dp", "tensor", None), P("dp", "tensor", None), P("tensor", None))
    return jax.shard_map(
        body,
        mesh=mesh,
        in_specs=placed,
        out_specs=(P("tensor", None), P("dp", "tensor", None), P("tensor", None)),
        check_vma=False,
    )
```

profile of v0, /device:TPU:1, one launch (start us, length us, event | category | flops | bytes accessed | tf_op | source)
XLA Modules:
  0.0 709.2 jit_solution(10508931071022394788)
XLA Ops:
  7.2 0.0 all-reduce.2.cloned.1.call-start
  7.2 32.1 %all_gather.3 = bf16[4096,64]{0,1:T(8,128)(2,1)S(1)} all-gather(bf16[256,64]{0,1:T(8,128)(2,1)} %param.5), channel_id=1, replica_groups=mesh['dp'=32,'tensor'=16] {'tensor'}, dimensions={0}, use_global_device_ids=true | all-gather | bytes 557056 | tf_op jit(solution)/shard_map/all_gather | solution.py:14
  39.3 0.0 copy-start
  39.3 0.0 copy-start.1
  39.3 2.2 fusion.9
  41.4 126.6 %psum.21 = f32[128,64]{0,1:T(8,128)S(1)} all-reduce(f32[128,64]{0,1:T(8,128)S(1)} %fusion.9), channel_id=1, replica_groups=mesh['dp'=32,'tensor'=16] {'dp'}, use_global_device_ids=true, to_apply=%region_0.0 | all-reduce | flops 8192 | bytes 65536 | tf_op jit(solution)/shard_map/psum | solution.py:17
  168.1 0.2 fusion.13
  168.3 39.0 %psum.22 = f32[64,64]{0,1:T(8,128)S(1)} all-reduce(f32[64,64]{0,1:T(8,128)S(1)} %fusion.13), channel_id=1, replica_groups=mesh['dp'=32,'tensor'=16] {'tensor'}, use_global_device_ids=true, to_apply=%region_1.0 | all-reduce | flops 4096 | bytes 32768 | tf_op jit(solution)/shard_map/psum | solution.py:18
  207.3 0.1 copy.7
  207.4 5.8 cholesky.16
  213.3 0.6 compare_reduce_fusion
  213.9 0.7 fusion.4
  214.6 4.9 custom-call.5
  219.5 0.3 convolution_convert_fusion
  219.7 0.0 copy-done
  219.7 0.0 copy-done.1
  219.8 1.4 fusion.7
  221.2 0.0 all-reduce.2.cloned.1.call-update
  221.2 477.3 %all-reduce.2.cloned.1.call-done = f32[4096,64]{0,1:T(8,128)} async-done(((f32[4096,64]{0,1:T(8,128)}), f32[4096,64]{0,1:T(8,128)}) %all-reduce.2.cloned.1.call-update) | async-done | bytes 1048592 | tf_op jit(solution)/shard_map/psum | solution.py:26
  698.5 0.0 copy-start.2
  698.5 1.4 broadcast_multiply_fusion
  699.9 0.6 constant_dynamic-slice_fusion
  700.6 0.0 copy-done.2
  700.6 1.8 fusion.1
  (2 shorter events, 0.0 us)
Async XLA Ops:
  7.2 691.3 %all-reduce.2.cloned.1.call-start = ((), (), s32[]{:S(2)}) async-start(), calls=%async_computation | async-start | bytes 2097152 | tf_op jit(solution)/shard_map/psum | solution.py:26
  39.3 180.5 %copy-start = (bf16[1,128,4096]{2,1,0:T(8,128)(2,1)S(1)}, bf16[1,128,4096]{2,1,0:T(8,128)(2,1)}, u32[]{:S(2)}) copy-start(bf16[1,128,4096]{2,1,0:T(8,128)(2,1)} %param.4) | copy-start | bytes 3145732
  39.3 180.5 %copy-start.1 = (bf16[1,128,4096]{2,1,0:T(8,128)(2,1)S(1)}, bf16[1,128,4096]{2,1,0:T(8,128)(2,1)}, u32[]{:S(2)}) copy-start(bf16[1,128,4096]{2,1,0:T(8,128)(2,1)} %param.3) | copy-start | bytes 3145732
  698.5 2.0 copy-start.2
Sparse Core Ops, SparseCore 0:
  221.3 477.1 all-reduce.1
where the time goes:
time: 709 us
  waiting for transfers between devices  477 us (67%)
  blocking collectives  198 us (28%)
  between operations  14.1 us (2%)
  other arithmetic  13.5 us (2%)
    psum x1, waiting for transfers between devices, body(): q_full = lax.psum(term, ('dp', 'tensor')) / replicas  477 us
    psum x1, blocking collectives, body(): p_sum = lax.psum(local_p, 'dp')  127 us
    psum x1, blocking collectives, body(): lax.psum(jnp.dot(p_sum.T, p_sum, precision=lax.Precision.HIGHEST), 'tensor')  39 us
    all_gather x1, blocking collectives, body(): lax.all_gather(q_start, 'tensor', axis=0, tiled=True)  32.1 us
  transfers between devices with their start and end apart: 1, of which 1 were waited for; matrix products, arithmetic and copies ran while one was open for 0% of the time, Pallas kernels for 0%

commit v1 on v0

v1 whole, which is shorter than its diff:
```python
import jax
import jax.numpy as jnp
from jax import lax
from jax.sharding import PartitionSpec as P

SIDE = 4
CHIPS = SIDE * SIDE
CORES = 2
DP = CHIPS * CORES
DEPTH = 16
R = 64
HIGH = lax.Precision.HIGHEST

PLANE = [[core + CORES * chip for chip in range(CHIPS)] for core in range(CORES)]
NEAR = [[4 * a + b for b in range(4)] for a in range(4)]
FAR = [[4 * a + b for a in range(4)] for b in range(4)]
SWAP = [(i, i ^ 1) for i in range(DP)]


def ring(a, b, n):
    return min((a - b) % n, (b - a) % n)


def factor_route():
    pairs = []
    for k in range(CHIPS):
        planes = sorted(range(DEPTH), key=lambda z: -ring(z, k, DEPTH))
        chips = sorted(
            range(CHIPS),
            key=lambda j: ring(j // SIDE, k // SIDE, SIDE) + ring(j % SIDE, k % SIDE, SIDE),
        )
        for z, j in zip(planes, chips):
            for core in range(CORES):
                pairs.append(((CORES * j + core) * DEPTH + k, (CORES * k + core) * DEPTH + z))
    return pairs


def share(x, axis, groups, size):
    return lax.all_to_all(
        jnp.broadcast_to(x[None], (size,) + x.shape), axis, 0, 0, axis_index_groups=groups
    )


def body(grad, error, q_start):
    core = lax.axis_index("dp") % CORES
    z = lax.axis_index("tensor")
    factor_t = lax.ppermute(q_start.T, ("dp", "tensor"), factor_route())
    corrected = (grad[0].astype(jnp.float32) + error[0].astype(jnp.float32)).astype(jnp.bfloat16)
    blocks = corrected.reshape(CORES, 64, CHIPS, 256).transpose(2, 0, 1, 3).reshape(DP, 64, 256)
    blocks = lax.all_to_all(blocks, "dp", 0, 0)
    total = jnp.sum(blocks.astype(jnp.float32), 0)
    part = lax.dot_general(
        total, factor_t.astype(jnp.float32), (((1,), (1,)), ((), ())), precision=HIGH
    )
    part = jnp.concatenate([part[:32], part[32:]], 1)
    packed_p = jnp.sum(share(part, "dp", PLANE, CHIPS), 0)
    p_mine = jnp.concatenate([packed_p[:, :R], packed_p[:, R:]], 0)
    t_part = lax.dot_general(p_mine, total, (((0,), (0,)), ((), ())), precision=HIGH)
    gram = lax.dot_general(p_mine, p_mine, (((0,), (0,)), ((), ())), precision=HIGH)
    gram = jnp.concatenate([gram[:32], gram[32:]], 1)
    keep = lax.dynamic_slice_in_dim(t_part, core * 128, 128, 1)
    give = lax.dynamic_slice_in_dim(t_part, (1 - core) * 128, 128, 1)
    got = lax.ppermute(jnp.concatenate([give, gram, packed_p], 0), "dp", SWAP)
    other_p = jnp.concatenate([got[96:, :R], got[96:, R:]], 0)
    p_sum = jnp.where(
        core == 0,
        jnp.concatenate([p_mine, other_p], 0),
        jnp.concatenate([other_p, p_mine], 0),
    )
    both = jnp.concatenate([keep, gram], 0) + got[:96]
    both = jnp.sum(share(both, "tensor", NEAR, 4), 0)
    both = jnp.sum(share(both, "tensor", FAR, 4), 0)
    gram = jnp.concatenate([both[64:, :R], both[64:, R:]], 0)
    lower = lax.linalg.cholesky(gram)
    inverse = lax.linalg.triangular_solve(
        lower, jnp.eye(R, dtype=jnp.float32), left_side=True, lower=True
    )
    q_block = jnp.dot(inverse, both[:64], precision=HIGH) / DP
    p_round = lax.dot_general(
        p_sum, inverse, (((1,), (1,)), ((), ())), precision=HIGH
    ).astype(jnp.bfloat16)
    q_blocks = share(q_block.astype(jnp.bfloat16), "dp", None, DP)
    q_round = q_blocks.transpose(1, 0, 2).reshape(R, DP * 128)
    full_update = jnp.dot(p_round, q_round, preferred_element_type=jnp.float32)
    new_error = (corrected.astype(jnp.float32) - full_update).astype(jnp.bfloat16)[None]
    q_mine = lax.dynamic_slice_in_dim(q_blocks, z * 2, 2, 0)
    q_mine = q_mine.transpose(0, 2, 1).reshape(256, R).astype(jnp.float32)
    return (full_update.astype(jnp.bfloat16), new_error, q_mine)


def solution(mesh):
    placed = (P("dp", "tensor", None), P("dp", "tensor", None), P("tensor", None))
    return jax.shard_map(
        body,
        mesh=mesh,
        in_specs=placed,
        out_specs=(P("tensor", None), P("dp", "tensor", None), P("tensor", None)),
        check_vma=False,
    )
```

time: 709 us -> 122 us (0.17)
  waiting for transfers between devices: 477 us -> 25.1 us
  blocking collectives: 198 us -> 34 us
  starting transfers between devices: 0.04 us -> 39.7 us
  between operations: 14.1 us -> 0.85 us
    psum x1 -> x0, waiting for transfers between devices: 477 us -> none  [body(): q_full = lax.psum(term, ('dp', 'tensor')) / replicas]
    psum x2 -> x0, blocking collectives: 166 us -> none  [the longest x1 127 us: body(): p_sum = lax.psum(local_p, 'dp')]
    all_to_all x0 -> x2, blocking collectives: none -> 34 us  [share(): lax.all_to_all(jnp.broadcast_to(x[None], (size,) + x.shape), axis, 0, 0,...]
    all_gather x1 -> x0, blocking collectives: 32.1 us -> none  [body(): lax.all_gather(q_start, 'tensor', axis=0, tiled=True)]
    all_to_all x0 -> x3, waiting for transfers between devices: none -> 23.2 us  [the longest x2 18.6 us: share(): lax.all_to_all(jnp.broadcast_to(x[None], (size,) + x.shape), axis, 0, 0,...]
    all_to_all x0 -> x3, starting transfers between devices: none -> 21.9 us  [the longest x2 11.3 us: share(): lax.all_to_all(jnp.broadcast_to(x[None], (size,) + x.shape), axis, 0, 0,...]
    ppermute x0 -> x2, starting transfers between devices: none -> 17.8 us  [the longest x1 13.6 us: body(): factor_t = lax.ppermute(q_start.T, ('dp', 'tensor'), factor_route())]
  transfers between devices with their start and end apart: 1 -> 5, of which waited for: 1 -> 5; matrix products, arithmetic and copies ran while one was open for 0% -> 0% of each run, Pallas kernels for 0% -> 0%
where the time goes in v1:
time: 122 us
  starting transfers between devices  39.7 us (33%)
  blocking collectives  34 us (28%)
  waiting for transfers between devices  25.1 us (21%)
  other arithmetic  15.1 us (12%)
  local copies, waits for them, and re-layouts  3.72 us (3%)
  matrix products  3.08 us (3%)
    all_to_all x2, blocking collectives, share(): lax.all_to_all(jnp.broadcast_to(x[None], (size,) + x.shape), axis, 0, 0,...  34 us
    all_to_all x2, waiting for transfers between devices, share(): lax.all_to_all(jnp.broadcast_to(x[None], (size,) + x.shape), axis, 0, 0,...  18.6 us
    ppermute x1, starting transfers between devices, body(): factor_t = lax.ppermute(q_start.T, ('dp', 'tensor'), factor_route())  13.6 us
    all_to_all x2, starting transfers between devices, share(): lax.all_to_all(jnp.broadcast_to(x[None], (size,) + x.shape), axis, 0, 0,...  11.3 us
    all_to_all x1, starting transfers between devices, body(): blocks = lax.all_to_all(blocks, 'dp', 0, 0)  10.6 us
    another operation x3, other arithmetic, body(): lower = lax.linalg.cholesky(gram)  6.53 us
    another operation x2, other arithmetic, body(): lax.linalg.triangular_solve(lower, jnp.eye(R, dtype=jnp.float32), left_si...  5.55 us
    all_to_all x1, waiting for transfers between devices, body(): blocks = lax.all_to_all(blocks, 'dp', 0, 0)  4.59 us
  transfers between devices with their start and end apart: 5, of which 5 were waited for; matrix products, arithmetic and copies ran while one was open for 0% of the time, Pallas kernels for 0%

profile of v1, /device:TPU:1, one launch (start us, length us, event | category | flops | bytes accessed | tf_op | source)
XLA Modules:
  0.0 121.5 jit_solution(15300207142112176815)
XLA Ops:
  0.6 1.8 %add_convert_fusion = bf16[1,128,4096]{2,1,0:T(8,128)(2,1)S(1)} fusion(bf16[1,128,4096]{2,1,0:T(8,128)(2,1)} %param.4, bf16[1,128,4096]{2,1,0:T(8,128)(2,1)} %param.3), kind=kLoop, calls=%fused_computation.3 | loop fusion | flops 2097152 | bytes 3145728 | tf_op jit(solution)/shard_map/convert_element_type | solution.py:48
  2.4 0.2 copy.25
  2.7 1.3 %copy.15 = bf16[2,64,16,256]{3,1,0,2:T(8,128)(2,1)} copy(bf16[2,64,16,256]{3,2,1,0:T(8,128)(2,1)S(1)} %bitcast.45) | data formatting | bytes 2097152 | tf_op jit(solution)/shard_map/convert_element_type | solution.py:48
  4.0 0.0 copy-start
  4.0 10.6 %all-to-all-start = ((bf16[32,64,256]{2,1,0:T(8,128)(2,1)}), bf16[32,64,256]{2,1,0:T(8,128)(2,1)S(1)}, u32[]{:S(2)}, u32[]{:S(2)}) async-start(bf16[32,64,256]{2,1,0:T(8,128)(2,1)} %bitcast.1), calls=%async_computation | async-start | bytes 2097152 | tf_op jit(solution)/shard_map/all_to_all | solution.py:50
  14.6 0.0 copy-done
  14.6 13.6 %collective-permute-start = (bf16[64,256]{1,0:T(8,128)(2,1)S(1)}, bf16[64,256]{1,0:T(8,128)(2,1)S(1)}, u32[]{:S(2)}, u32[]{:S(2)}) collective-permute-start(bf16[64,256]{1,0:T(8,128)(2,1)S(1)} %bitcast.46), channel_id=1, source_target_pairs={{0,8},{16,24},{32,7},{48,23},{96,9},{112,25},{128,6},{144,22},{384... | collective-permute-start | bytes 98312 | tf_op jit(solution)/shard_map/ppermute | solution.py:47
  28.2 4.6 %all-to-all-done = bf16[32,64,256]{2,1,0:T(8,128)(2,1)S(1)} async-done(((bf16[32,64,256]{2,1,0:T(8,128)(2,1)}), bf16[32,64,256]{2,1,0:T(8,128)(2,1)S(1)}, u32[]{:S(2)}, u32[]{:S(2)}) %all-to-all-start) | async-done | bytes 1048608 | tf_op jit(solution)/shard_map/all_to_all | solution.py:50
  32.8 0.2 convert_reduce_fusion
  32.9 1.0 collective-permute-done
  33.9 0.2 fusion.37
  34.1 0.1 pad_maximum_fusion.5
  34.2 0.7 broadcast_in_dim.10
  34.9 3.5 %all-to-all-start.1 = ((f32[16,32,128]{2,1,0:T(8,128)}), f32[16,32,128]{2,1,0:T(8,128)S(1)}, u32[]{:S(2)}, u32[]{:S(2)}) async-start(f32[16,32,128]{2,1,0:T(8,128)} %broadcast_in_dim.10), calls=%async_computation.1 | async-start | bytes 524288 | tf_op jit(solution)/shard_map/all_to_all | solution.py:39
  38.5 7.3 %all-to-all-done.1 = f32[16,32,128]{2,1,0:T(8,128)S(1)} async-done(((f32[16,32,128]{2,1,0:T(8,128)}), f32[16,32,128]{2,1,0:T(8,128)S(1)}, u32[]{:S(2)}, u32[]{:S(2)}) %all-to-all-start.1) | async-done | bytes 262176 | tf_op jit(solution)/shard_map/all_to_all | solution.py:39
  45.8 0.1 fusion.34
  45.9 0.2 fusion.25
  46.1 0.3 fusion.26
  46.4 0.1 pad_maximum_fusion
  46.5 4.2 %collective-permute-start.1 = (f32[128,128]{1,0:T(8,128)S(1)}, f32[128,128]{1,0:T(8,128)S(1)}, u32[]{:S(2)}, u32[]{:S(2)}) collective-permute-start(f32[128,128]{1,0:T(8,128)S(1)} %pad_maximum_fusion), channel_id=1, source_target_pairs={{0,16},{16,0},{32,48},{48,32},{64,80},{80,64},{96,112},{112,96},{1... | collective-permute-start | bytes 196616 | tf_op jit(solution)/shard_map/ppermute | solution.py:63
  50.7 0.9 collective-permute-done.1
  51.6 0.1 slice_add_fusion
  51.7 8.6 %all_to_all.25 = f32[4,96,128]{2,1,0:T(8,128)S(1)} all-to-all(f32[4,96,128]{2,1,0:T(8,128)S(1)} %broadcast_in_dim.11), channel_id=1, replica_groups={{0,1,2,3},{4,5,6,7},{8,9,10,11},{12,13,14,15},{16,17,18,19},{20,21,22,2..., dimensions={0} | all-to-all | bytes 393216 | tf_op jit(solution)/shard_map/all_to_all | solution.py:39
  60.3 25.5 %all_to_all.26 = f32[4,96,128]{2,1,0:T(8,128)S(1)} all-to-all(f32[4,96,128]{2,1,0:T(8,128)S(1)} %broadcast_in_dim.12), channel_id=1, replica_groups={{0,4,8,12},{1,5,9,13},{2,6,10,14},{3,7,11,15},{16,20,24,28},{17,21,25,2..., dimensions={0} | all-to-all | bytes 393216 | tf_op jit(solution)/shard_map/all_to_all | solution.py:39
  85.8 0.1 fusion.31
  85.9 0.1 copy.22
  86.0 0.1 copy.21
  86.0 0.1 pad_maximum_fusion.2
  86.1 0.1 copy.18
  86.2 0.1 fusion.23
  86.3 5.9 %cholesky.17 = f32[64,64]{1,0:T(8,128)S(1)} custom-call(f32[64,64]{1,0:T(8,128)S(1)} %fusion.23), custom_call_target="Cholesky" | custom-call | tf_op jit(solution)/shard_map/cholesky | solution.py:74
  92.2 0.6 compare_reduce_fusion
  92.8 0.7 fusion.19
  93.5 4.9 %custom-call.5 = f32[1,64,64]{1,2,0:T(8,128)S(1)} custom-call(f32[1,64,64]{2,1,0:T(8,128)S(1)} %fusion.19), custom_call_target="InvertDiagBlocksLowerTriangular" | custom-call | tf_op jit(solution)/shard_map/triangular_solve | solution.py:75
  98.4 0.2 fusion.21
  98.6 0.2 fusion.1
  98.8 0.9 broadcast_in_dim.13
  99.7 7.8 %all-to-all-start.4 = ((bf16[32,64,128]{2,1,0:T(8,128)(2,1)}), bf16[32,64,128]{2,1,0:T(8,128)(2,1)S(1)}, u32[]{:S(2)}, u32[]{:S(2)}) async-start(bf16[32,64,128]{2,1,0:T(8,128)(2,1)} %broadcast_in_dim.13), calls=%async_computation.4 | async-start | bytes 1048576 | tf_op jit(solution)/shard_map/all_to_all | solution.py:39
  107.5 0.1 fusion.30
  107.6 0.2 convolution_convert_fusion
  107.8 11.3 %all-to-all-done.4 = bf16[32,64,128]{2,1,0:T(8,128)(2,1)S(1)} async-done(((bf16[32,64,128]{2,1,0:T(8,128)(2,1)}), bf16[32,64,128]{2,1,0:T(8,128)(2,1)S(1)}, u32[]{:S(2)}, u32[]{:S(2)}) %all-to-all-start.4) | async-done | bytes 524320 | tf_op jit(solution)/shard_map/all_to_all | solution.py:39
  119.1 1.8 %fusion.2 = (bf16[1,128,4096]{2,1,0:T(8,128)(2,1)}, bf16[128,4096]{1,0:T(8,128)(2,1)}) fusion(bf16[1,128,4096]{2,1,0:T(8,128)(2,1)S(1)} %add_convert_fusion, bf16[128,64]{0,1:T(8,128)(2,1)S(1)} %convolution_convert_fusion, bf16[32,64,128]{2,1,0:T(8,128)(2,1)S(1)} %all-to-all-done.4), kind=kOutput, calls=%fused_computation.7 | convolution fusion | flops 69206016 | bytes 3686400 | tf_op jit(solution)/shard_map/dot_general | solution.py:84
  120.9 0.6 copy_bitcast_fusion
  (9 shorter events, 0.1 us)
Async XLA Ops:
  4.0 10.6 %copy-start = (bf16[256,64]{0,1:T(8,128)(2,1)S(1)}, bf16[256,64]{0,1:T(8,128)(2,1)}, u32[]{:S(2)}) copy-start(bf16[256,64]{0,1:T(8,128)(2,1)} %param.5) | copy-start | bytes 98308
  4.0 28.8 %all-to-all-start = ((bf16[32,64,256]{2,1,0:T(8,128)(2,1)}), bf16[32,64,256]{2,1,0:T(8,128)(2,1)S(1)}, u32[]{:S(2)}, u32[]{:S(2)}) async-start(bf16[32,64,256]{2,1,0:T(8,128)(2,1)} %bitcast.1), calls=%async_computation | async-start | bytes 2097152 | tf_op jit(solution)/shard_map/all_to_all | solution.py:50
  14.6 19.3 %collective-permute-start = (bf16[64,256]{1,0:T(8,128)(2,1)S(1)}, bf16[64,256]{1,0:T(8,128)(2,1)S(1)}, u32[]{:S(2)}, u32[]{:S(2)}) collective-permute-start(bf16[64,256]{1,0:T(8,128)(2,1)S(1)} %bitcast.46), channel_id=1, source_target_pairs={{0,8},{16,24},{32,7},{48,23},{96,9},{112,25},{128,6},{144,22},{384... | collective-permute-start | bytes 98312 | tf_op jit(solution)/shard_map/ppermute | solution.py:47
  34.9 10.9 %all-to-all-start.1 = ((f32[16,32,128]{2,1,0:T(8,128)}), f32[16,32,128]{2,1,0:T(8,128)S(1)}, u32[]{:S(2)}, u32[]{:S(2)}) async-start(f32[16,32,128]{2,1,0:T(8,128)} %broadcast_in_dim.10), calls=%async_computation.1 | async-start | bytes 524288 | tf_op jit(solution)/shard_map/all_to_all | solution.py:39
  46.5 5.1 %collective-permute-start.1 = (f32[128,128]{1,0:T(8,128)S(1)}, f32[128,128]{1,0:T(8,128)S(1)}, u32[]{:S(2)}, u32[]{:S(2)}) collective-permute-start(f32[128,128]{1,0:T(8,128)S(1)} %pad_maximum_fusion), channel_id=1, source_target_pairs={{0,16},{16,0},{32,48},{48,32},{64,80},{80,64},{96,112},{112,96},{1... | collective-permute-start | bytes 196616 | tf_op jit(solution)/shard_map/ppermute | solution.py:63
  99.7 19.4 %all-to-all-start.4 = ((bf16[32,64,128]{2,1,0:T(8,128)(2,1)}), bf16[32,64,128]{2,1,0:T(8,128)(2,1)S(1)}, u32[]{:S(2)}, u32[]{:S(2)}) async-start(bf16[32,64,128]{2,1,0:T(8,128)(2,1)} %broadcast_in_dim.13), calls=%async_computation.4 | async-start | bytes 1048576 | tf_op jit(solution)/shard_map/all_to_all | solution.py:39

commit v2 on v1

--- a/solution.py
+++ b/solution.py
@@ -1,6 +1,7 @@
 import jax
 import jax.numpy as jnp
 from jax import lax
+from jax.experimental import pallas as pl
 from jax.sharding import PartitionSpec as P
 
 SIDE = 4
@@ -41,6 +42,56 @@
     )
 
 
+def splat_row(x, row):
+    return jnp.broadcast_to(x[row : row + 1, :], (8, 128))
+
+
+def inverse_factor(gram):
+    rows = lax.broadcasted_iota(jnp.int32, (R, R), 0)
+    eye = (rows == lax.broadcasted_iota(jnp.int32, (R, R), 1)).astype(jnp.float32)
+    both = jnp.concatenate([gram, eye], 1)
+    n = R // 8
+    strips = [both[8 * t : 8 * t + 8] for t in range(n)]
+    sub = lax.broadcasted_iota(jnp.int32, (8, 128), 0)
+    scaled = []
+    for s in range(n):
+        cols = [
+            [jnp.broadcast_to(strips[t][:, 8 * s + j : 8 * s + j + 1], (8, 128)) for t in range(s, n)]
+            for j in range(8)
+        ]
+        done = jnp.zeros((8, 128), jnp.float32)
+        for j in range(8):
+            pivot, row = splat_row(cols[j][0], j), splat_row(strips[s], j)
+            root = lax.rsqrt(pivot)
+            root = root * (1.5 - 0.5 * pivot * root * root)
+            done = jnp.where(sub == j, row * root, done)
+            factors = [c * (root * root) for c in cols[j]]
+            factors[0] = jnp.where(sub > j, factors[0], 0.0)
+            for i in range(j + 1, 8):
+                entry = splat_row(cols[i][0], j)
+                cols[i] = [c - f * entry for c, f in zip(cols[i], factors)]
+            for t in range(s, n):
+                strips[t] = strips[t] - factors[t - s] * row
+        scaled.append(done)
+    return jnp.concatenate(scaled, 0)[:, R:]
+
+
+def factor_kernel(far_ref, p_ref, q_ref, p_round_ref):
+    both = far_ref[0] + far_ref[1] + (far_ref[2] + far_ref[3])
+    inverse = inverse_factor(jnp.concatenate([both[64:, :R], both[64:, R:]], 0))
+    q_block = jnp.dot(
+        inverse, both[:64], precision=HIGH, preferred_element_type=jnp.float32
+    ) * (1.0 / DP)
+    q_ref[...] = jnp.broadcast_to(q_block.astype(jnp.bfloat16)[None], q_ref.shape)
+    p_round_ref[...] = lax.dot_general(
+        p_ref[...],
+        inverse,
+        (((1,), (1,)), ((), ())),
+        precision=HIGH,
+        preferred_element_type=jnp.float32,
+    ).astype(jnp.bfloat16)
+
+
 def body(grad, error, q_start):
     core = lax.axis_index("dp") % CORES
     z = lax.axis_index("tensor")
@@ -69,17 +120,14 @@
     )
     both = jnp.concatenate([keep, gram], 0) + got[:96]
     both = jnp.sum(share(both, "tensor", NEAR, 4), 0)
-    both = jnp.sum(share(both, "tensor", FAR, 4), 0)
-    gram = jnp.concatenate([both[64:, :R], both[64:, R:]], 0)
-    lower = lax.linalg.cholesky(gram)
-    inverse = lax.linalg.triangular_solve(
-        lower, jnp.eye(R, dtype=jnp.float32), left_side=True, lower=True
-    )
-    q_block = jnp.dot(inverse, both[:64], precision=HIGH) / DP
-    p_round = lax.dot_general(
-        p_sum, inverse, (((1,), (1,)), ((), ())), precision=HIGH
-    ).astype(jnp.bfloat16)
-    q_blocks = share(q_block.astype(jnp.bfloat16), "dp", None, DP)
+    q_blocks, p_round = pl.pallas_call(
+        factor_kernel,
+        out_shape=(
+            jax.ShapeDtypeStruct((DP, R, 128), jnp.bfloat16),
+            jax.ShapeDtypeStruct((128, R), jnp.bfloat16),
+        ),
+    )(share(both, "tensor", FAR, 4), p_sum)
+    q_blocks = lax.all_to_all(q_blocks, "dp", 0, 0)
     q_round = q_blocks.transpose(1, 0, 2).reshape(R, DP * 128)
     full_update = jnp.dot(p_round, q_round, preferred_element_type=jnp.float32)
     new_error = (corrected.astype(jnp.float32) - full_update).astype(jnp.bfloat16)[None]

time: 122 us -> 114 us (0.934)
  blocking collectives: 34 us -> 8.57 us
  starting transfers between devices: 39.7 us -> 52.3 us
  waiting for transfers between devices: 25.1 us -> 37.3 us
  other arithmetic: 15.1 us -> 3.48 us
  Pallas kernels: 0 us -> 4.39 us
    all_to_all x2 -> x1, blocking collectives: 34 us -> 8.57 us  [share(): lax.all_to_all(jnp.broadcast_to(x[None], (size,) + x.shape), axis, 0, 0,...]
    another operation x5 -> x0, other arithmetic: 12.1 us -> none  [the longest x3 6.53 us: body(): lower = lax.linalg.cholesky(gram)]
    all_to_all x0 -> x1, waiting for transfers between devices: none -> 11.6 us  [body(): q_blocks = lax.all_to_all(q_blocks, 'dp', 0, 0)]
    all_to_all x0 -> x1, starting transfers between devices: none -> 9.37 us  [body(): q_blocks = lax.all_to_all(q_blocks, 'dp', 0, 0)]
    pallas_call x0 -> x1, Pallas kernels: none -> 4.39 us  [body(): pl.pallas_call(factor_kernel, out_shape=(jax.ShapeDtypeStruct((DP, R, 128...]
    all_to_all x2, starting transfers between devices: 11.3 us -> 14.6 us  [share(): lax.all_to_all(jnp.broadcast_to(x[None], (size,) + x.shape), axis, 0, 0,...]
  transfers between devices with their start and end apart: 5 -> 6, of which waited for: 5 -> 6; matrix products, arithmetic and copies ran while one was open for 0% -> 1% of each run, Pallas kernels for 0% -> 0%
where the time goes in v2:
time: 114 us; the launch traced here: 113 us
  starting transfers between devices  52.3 us (46%)
  waiting for transfers between devices  37.3 us (33%)
  blocking collectives  8.57 us (8%)
  Pallas kernels  4.39 us (4%)
  local copies, waits for them, and re-layouts  3.85 us (3%)
  other arithmetic  3.48 us (3%)
  matrix products  2.39 us (2%)
    all_to_all x2, waiting for transfers between devices, share(): lax.all_to_all(jnp.broadcast_to(x[None], (size,) + x.shape), axis, 0, 0,...  19.2 us
    all_to_all x2, starting transfers between devices, share(): lax.all_to_all(jnp.broadcast_to(x[None], (size,) + x.shape), axis, 0, 0,...  14.6 us
    ppermute x1, starting transfers between devices, body(): factor_t = lax.ppermute(q_start.T, ('dp', 'tensor'), factor_route())  13.6 us
    all_to_all x1, waiting for transfers between devices, body(): q_blocks = lax.all_to_all(q_blocks, 'dp', 0, 0)  11.6 us
    all_to_all x1, starting transfers between devices, body(): blocks = lax.all_to_all(blocks, 'dp', 0, 0)  10.6 us
    all_to_all x1, starting transfers between devices, body(): q_blocks = lax.all_to_all(q_blocks, 'dp', 0, 0)  9.37 us
    all_to_all x1, blocking collectives, share(): lax.all_to_all(jnp.broadcast_to(x[None], (size,) + x.shape), axis, 0, 0,...  8.57 us
    all_to_all x1, waiting for transfers between devices, body(): blocks = lax.all_to_all(blocks, 'dp', 0, 0)  4.59 us
  transfers between devices with their start and end apart: 6, of which 6 were waited for; matrix products, arithmetic and copies ran while one was open for 1% of the time, Pallas kernels for 0%

profile of v2, /device:TPU:1, one launch (start us, length us, event | category | flops | bytes accessed | tf_op | source)
XLA Modules:
  0.0 113.1 jit_solution(3295698307083995907)
XLA Ops:
  0.6 1.8 %add_convert_fusion = bf16[1,128,4096]{2,1,0:T(8,128)(2,1)S(1)} fusion(bf16[1,128,4096]{2,1,0:T(8,128)(2,1)} %param.4, bf16[1,128,4096]{2,1,0:T(8,128)(2,1)} %param.3), kind=kLoop, calls=%fused_computation.3 | loop fusion | flops 2097152 | bytes 3145728 | tf_op jit(solution)/shard_map/convert_element_type | solution.py:99
  2.4 0.2 copy.14
  2.7 1.3 %copy.9 = bf16[2,64,16,256]{3,1,0,2:T(8,128)(2,1)} copy(bf16[2,64,16,256]{3,2,1,0:T(8,128)(2,1)S(1)} %bitcast.34) | data formatting | bytes 2097152 | tf_op jit(solution)/shard_map/convert_element_type | solution.py:99
  4.0 0.0 copy-start.2
  4.0 10.6 %all-to-all-start = ((bf16[32,64,256]{2,1,0:T(8,128)(2,1)}), bf16[32,64,256]{2,1,0:T(8,128)(2,1)S(1)}, u32[]{:S(2)}, u32[]{:S(2)}) async-start(bf16[32,64,256]{2,1,0:T(8,128)(2,1)} %bitcast.1), calls=%async_computation | async-start | bytes 2097152 | tf_op jit(solution)/shard_map/all_to_all | solution.py:101
  14.6 0.0 copy-done.2
  14.6 13.6 %collective-permute-start = (bf16[64,256]{1,0:T(8,128)(2,1)S(1)}, bf16[64,256]{1,0:T(8,128)(2,1)S(1)}, u32[]{:S(2)}, u32[]{:S(2)}) collective-permute-start(bf16[64,256]{1,0:T(8,128)(2,1)S(1)} %bitcast.35), channel_id=1, source_target_pairs={{0,8},{16,24},{32,7},{48,23},{96,9},{112,25},{128,6},{144,22},{384... | collective-permute-start | bytes 98312 | tf_op jit(solution)/shard_map/ppermute | solution.py:98
  28.2 4.6 %all-to-all-done = bf16[32,64,256]{2,1,0:T(8,128)(2,1)S(1)} async-done(((bf16[32,64,256]{2,1,0:T(8,128)(2,1)}), bf16[32,64,256]{2,1,0:T(8,128)(2,1)S(1)}, u32[]{:S(2)}, u32[]{:S(2)}) %all-to-all-start) | async-done | bytes 1048608 | tf_op jit(solution)/shard_map/all_to_all | solution.py:101
  32.8 0.2 convert_reduce_fusion
  32.9 1.0 collective-permute-done
  33.9 0.2 fusion.15
  34.1 0.1 pad_maximum_fusion.4
  34.2 0.7 broadcast_in_dim.8
  34.9 3.5 %all-to-all-start.1 = ((f32[16,32,128]{2,1,0:T(8,128)}), f32[16,32,128]{2,1,0:T(8,128)S(1)}, u32[]{:S(2)}, u32[]{:S(2)}) async-start(f32[16,32,128]{2,1,0:T(8,128)} %broadcast_in_dim.8), calls=%async_computation.1 | async-start | bytes 524288 | tf_op jit(solution)/shard_map/all_to_all | solution.py:40
  38.5 7.3 %all-to-all-done.1 = f32[16,32,128]{2,1,0:T(8,128)S(1)} async-done(((f32[16,32,128]{2,1,0:T(8,128)}), f32[16,32,128]{2,1,0:T(8,128)S(1)}, u32[]{:S(2)}, u32[]{:S(2)}) %all-to-all-start.1) | async-done | bytes 262176 | tf_op jit(solution)/shard_map/all_to_all | solution.py:40
  45.8 0.1 fusion.12
  45.9 0.2 fusion.5
  46.1 0.3 fusion.6
  46.4 0.1 pad_maximum_fusion
  46.5 4.2 %collective-permute-start.1 = (f32[128,128]{1,0:T(8,128)S(1)}, f32[128,128]{1,0:T(8,128)S(1)}, u32[]{:S(2)}, u32[]{:S(2)}) collective-permute-start(f32[128,128]{1,0:T(8,128)S(1)} %pad_maximum_fusion), channel_id=1, source_target_pairs={{0,16},{16,0},{32,48},{48,32},{64,80},{80,64},{96,112},{112,96},{1... | collective-permute-start | bytes 196616 | tf_op jit(solution)/shard_map/ppermute | solution.py:114
  50.7 0.9 collective-permute-done.1
  51.6 0.1 slice_add_fusion
  51.7 8.6 %all_to_all.25 = f32[4,96,128]{2,1,0:T(8,128)S(1)} all-to-all(f32[4,96,128]{2,1,0:T(8,128)S(1)} %broadcast_in_dim.9), channel_id=1, replica_groups={{0,1,2,3},{4,5,6,7},{8,9,10,11},{12,13,14,15},{16,17,18,19},{20,21,22,2..., dimensions={0} | all-to-all | bytes 393216 | tf_op jit(solution)/shard_map/all_to_all | solution.py:40
  60.3 0.7 broadcast_in_dim.10
  61.0 11.1 %all-to-all-start.3 = ((f32[4,96,128]{2,1,0:T(8,128)}), f32[4,96,128]{2,1,0:T(8,128)S(1)}, u32[]{:S(2)}, u32[]{:S(2)}) async-start(f32[4,96,128]{2,1,0:T(8,128)} %broadcast_in_dim.10), calls=%async_computation.3 | async-start | bytes 393216 | tf_op jit(solution)/shard_map/all_to_all | solution.py:40
  72.1 0.1 fusion.9
  72.1 0.6 maximum_select_fusion.p_ref
  72.8 11.9 %all-to-all-done.3.far_ref = f32[4,96,128]{2,1,0:T(8,128)S(1)} async-done(((f32[4,96,128]{2,1,0:T(8,128)}), f32[4,96,128]{2,1,0:T(8,128)S(1)}, u32[]{:S(2)}, u32[]{:S(2)}) %all-to-all-start.3) | async-done | bytes 196640 | tf_op jit(solution)/shard_map/all_to_all | solution.py:40
  84.7 0.0 copy-start
  84.7 0.7 copy-done
  85.4 4.4 %shard_map.58 = (bf16[32,64,128]{2,1,0:T(8,128)(2,1)}, bf16[128,64]{1,0:T(8,128)(2,1)}) custom-call(f32[4,96,128]{2,1,0:T(8,128)} %copy-done, f32[128,64]{1,0:T(8,128)} %maximum_select_fusion.p_ref), custom_call_target="tpu_custom_call" | custom-call | tf_op jit(solution)/shard_map/pallas_call | solution.py:123
  89.8 0.0 copy-start.1
  89.8 9.4 %all-to-all-start.4 = ((bf16[32,64,128]{2,1,0:T(8,128)(2,1)}), bf16[32,64,128]{2,1,0:T(8,128)(2,1)S(1)}, u32[]{:S(2)}, u32[]{:S(2)}) async-start(bf16[32,64,128]{2,1,0:T(8,128)(2,1)} %get-tuple-element.6), calls=%async_computation.4 | async-start | bytes 1048576 | tf_op jit(solution)/shard_map/all_to_all | solution.py:130
  99.2 11.6 %all-to-all-done.4 = bf16[32,64,128]{2,1,0:T(8,128)(2,1)S(1)} async-done(((bf16[32,64,128]{2,1,0:T(8,128)(2,1)}), bf16[32,64,128]{2,1,0:T(8,128)(2,1)S(1)}, u32[]{:S(2)}, u32[]{:S(2)}) %all-to-all-start.4) | async-done | bytes 524320 | tf_op jit(solution)/shard_map/all_to_all | solution.py:130
  110.8 0.0 copy-done.1
  110.8 1.7 %fusion.1 = (bf16[1,128,4096]{2,1,0:T(8,128)(2,1)}, bf16[128,4096]{1,0:T(8,128)(2,1)}) fusion(bf16[1,128,4096]{2,1,0:T(8,128)(2,1)S(1)} %add_convert_fusion, bf16[128,64]{1,0:T(8,128)(2,1)S(1)} %copy-done.1, bf16[32,64,128]{2,1,0:T(8,128)(2,1)S(1)} %all-to-all-done.4), kind=kOutput, calls=%fused_computation.4 | convolution fusion | flops 69206016 | bytes 3686400 | tf_op jit(solution)/shard_map/dot_general | solution.py:132
  112.5 0.6 copy_bitcast_fusion
  (6 shorter events, 0.1 us)
Async XLA Ops:
  4.0 10.6 %copy-start.2 = (bf16[256,64]{0,1:T(8,128)(2,1)S(1)}, bf16[256,64]{0,1:T(8,128)(2,1)}, u32[]{:S(2)}) copy-start(bf16[256,64]{0,1:T(8,128)(2,1)} %param.5) | copy-start | bytes 98308
  4.0 28.8 %all-to-all-start = ((bf16[32,64,256]{2,1,0:T(8,128)(2,1)}), bf16[32,64,256]{2,1,0:T(8,128)(2,1)S(1)}, u32[]{:S(2)}, u32[]{:S(2)}) async-start(bf16[32,64,256]{2,1,0:T(8,128)(2,1)} %bitcast.1), calls=%async_computation | async-start | bytes 2097152 | tf_op jit(solution)/shard_map/all_to_all | solution.py:101
  14.6 19.3 %collective-permute-start = (bf16[64,256]{1,0:T(8,128)(2,1)S(1)}, bf16[64,256]{1,0:T(8,128)(2,1)S(1)}, u32[]{:S(2)}, u32[]{:S(2)}) collective-permute-start(bf16[64,256]{1,0:T(8,128)(2,1)S(1)} %bitcast.35), channel_id=1, source_target_pairs={{0,8},{16,24},{32,7},{48,23},{96,9},{112,25},{128,6},{144,22},{384... | collective-permute-start | bytes 98312 | tf_op jit(solution)/shard_map/ppermute | solution.py:98
  34.9 10.9 %all-to-all-start.1 = ((f32[16,32,128]{2,1,0:T(8,128)}), f32[16,32,128]{2,1,0:T(8,128)S(1)}, u32[]{:S(2)}, u32[]{:S(2)}) async-start(f32[16,32,128]{2,1,0:T(8,128)} %broadcast_in_dim.8), calls=%async_computation.1 | async-start | bytes 524288 | tf_op jit(solution)/shard_map/all_to_all | solution.py:40
  46.5 5.1 %collective-permute-start.1 = (f32[128,128]{1,0:T(8,128)S(1)}, f32[128,128]{1,0:T(8,128)S(1)}, u32[]{:S(2)}, u32[]{:S(2)}) collective-permute-start(f32[128,128]{1,0:T(8,128)S(1)} %pad_maximum_fusion), channel_id=1, source_target_pairs={{0,16},{16,0},{32,48},{48,32},{64,80},{80,64},{96,112},{112,96},{1... | collective-permute-start | bytes 196616 | tf_op jit(solution)/shard_map/ppermute | solution.py:114
  61.0 23.7 %all-to-all-start.3 = ((f32[4,96,128]{2,1,0:T(8,128)}), f32[4,96,128]{2,1,0:T(8,128)S(1)}, u32[]{:S(2)}, u32[]{:S(2)}) async-start(f32[4,96,128]{2,1,0:T(8,128)} %broadcast_in_dim.10), calls=%async_computation.3 | async-start | bytes 393216 | tf_op jit(solution)/shard_map/all_to_all | solution.py:40
  84.7 0.7 copy-start
  89.8 21.0 %copy-start.1 = (bf16[128,64]{1,0:T(8,128)(2,1)S(1)}, bf16[128,64]{1,0:T(8,128)(2,1)}, u32[]{:S(2)}) copy-start(bf16[128,64]{1,0:T(8,128)(2,1)} %get-tuple-element.5) | copy-start | bytes 49156
  89.8 21.0 %all-to-all-start.4 = ((bf16[32,64,128]{2,1,0:T(8,128)(2,1)}), bf16[32,64,128]{2,1,0:T(8,128)(2,1)S(1)}, u32[]{:S(2)}, u32[]{:S(2)}) async-start(bf16[32,64,128]{2,1,0:T(8,128)(2,1)} %get-tuple-element.6), calls=%async_computation.4 | async-start | bytes 1048576 | tf_op jit(solution)/shard_map/all_to_all | solution.py:130

commit v3 on v2

v3 whole, which is shorter than its diff:
```python
import jax
import jax.numpy as jnp
from jax import lax
from jax.experimental import pallas as pl
from jax.experimental.pallas import tpu as pltpu
from jax.sharding import PartitionSpec as P

SIDE = 4
CHIPS = SIDE * SIDE
CORES = 2
DP = CHIPS * CORES
DEPTH = 16
ROWS = 128
HALF = ROWS // CORES
D = 4096
COLS = D // CHIPS
R = 64
HIGH = lax.Precision.HIGHEST
F32, BF16 = jnp.float32, jnp.bfloat16

PLANE = [[core + CORES * chip for chip in range(CHIPS)] for core in range(CORES)]
NEAR = [[4 * a + b for b in range(4)] for a in range(4)]
FAR = [[4 * a + b for a in range(4)] for b in range(4)]
SWAP = [(i, i ^ 1) for i in range(DP)]
PAIRED = [[i * DEPTH + 2 * a + b for b in range(2) for i in range(DP)] for a in range(DEPTH // 2)]


def ring(a, b, n):
    return min((a - b) % n, (b - a) % n)


def factor_route():
    pairs = []
    for k in range(CHIPS):
        planes = sorted(range(DEPTH), key=lambda z: -ring(z, k, DEPTH))
        chips = sorted(
            range(CHIPS),
            key=lambda j: ring(j // SIDE, k // SIDE, SIDE) + ring(j % SIDE, k % SIDE, SIDE),
        )
        for z, j in zip(planes, chips):
            for core in range(CORES):
                pairs.append(((CORES * j + core) * DEPTH + k, (CORES * k + core) * DEPTH + z))
    return pairs


def shape(*dims, dtype=F32):
    return jax.ShapeDtypeStruct(dims, dtype)


def pack(x):
    return jnp.concatenate([x[:32, :R], x[32:, :R]], 1)


def unpack(x):
    return jnp.concatenate([x[:, :R], x[:, R:]], 0)


def dot(a, b, over, **kw):
    return lax.dot_general(a, b, (over, ((), ())), preferred_element_type=F32, **kw)


def correct_kernel(grad_ref, error_ref, out_ref):
    x = (grad_ref[0].astype(F32) + error_ref[0].astype(F32)).astype(BF16)
    for k in range(out_ref.shape[0] // CORES):
        for c in range(CORES):
            out_ref[CORES * k + c] = x[HALF * c : HALF * (c + 1), COLS * k : COLS * (k + 1)]


def sketch_kernel(blocks_ref, factor_ref, total_ref, share_ref):
    total = blocks_ref[0].astype(F32)
    for i in range(1, DP):
        total = total + blocks_ref[i].astype(F32)
    total_ref[...] = total
    part = pack(dot(total, factor_ref[...].astype(F32), ((1,), (1,)), precision=HIGH))
    share_ref[...] = jnp.broadcast_to(part[None], share_ref.shape)


def basis_kernel(share_ref, total_ref, give_ref, keep_ref):
    packed = share_ref[0]
    for k in range(1, CHIPS):
        packed = packed + share_ref[k]
    p = unpack(packed)
    first = lax.rem(lax.axis_index("dp"), CORES) == 0
    left = dot(p, total_ref[:, :128], ((0,), (0,)), precision=HIGH)
    right = dot(p, total_ref[:, 128:], ((0,), (0,)), precision=HIGH)
    gram = pack(dot(p, p, ((0,), (0,)), precision=HIGH))
    keep_ref[:R] = jnp.where(first, left, right)
    give_ref[:R] = jnp.where(first, right, left)
    for ref in (keep_ref, give_ref):
        ref[R : R + 32] = gram
        ref[R + 32 :] = packed


def near_kernel(keep_ref, got_ref, share_ref, p_ref):
    both = keep_ref[:R] + got_ref[:R]
    gram = keep_ref[R : R + 32] + got_ref[R : R + 32]
    for half in range(2):
        part = pack(both[:, R * half : R * (half + 1)])
        for m in (half, half + 2):
            share_ref[m, :32] = part
            share_ref[m, 32:] = gram
    first = lax.rem(lax.axis_index("dp"), CORES) == 0
    mine, other = unpack(keep_ref[R + 32 :]), unpack(got_ref[R + 32 :])
    p_ref[:HALF] = jnp.where(first, mine, other)
    p_ref[HALF:] = jnp.where(first, other, mine)


def far_kernel(near_ref, share_ref):
    both = near_ref[0] + near_ref[1] + (near_ref[2] + near_ref[3])
    share_ref[...] = jnp.broadcast_to(both[None], share_ref.shape)


def splat_row(x, row):
    return jnp.broadcast_to(x[row : row + 1, :], (8, 128))


def inverse_factor(gram):
    rows = lax.broadcasted_iota(jnp.int32, (R, R), 0)
    eye = (rows == lax.broadcasted_iota(jnp.int32, (R, R), 1)).astype(F32)
    both = jnp.concatenate([gram, eye], 1)
    n = R // 8
    strips = [both[8 * t : 8 * t + 8] for t in range(n)]
    sub = lax.broadcasted_iota(jnp.int32, (8, 128), 0)
    scaled = []
    for s in range(n):
        cols = [
            [jnp.broadcast_to(strips[t][:, 8 * s + j : 8 * s + j + 1], (8, 128)) for t in range(s, n)]
            for j in range(8)
        ]
        done = jnp.zeros((8, 128), F32)
        for j in range(8):
            pivot, row = splat_row(cols[j][0], j), splat_row(strips[s], j)
            root = lax.rsqrt(pivot)
            root = root * (1.5 - 0.5 * pivot * root * root)
            done = jnp.where(sub == j, row * root, done)
            factors = [c * (root * root) for c in cols[j]]
            factors[0] = jnp.where(sub > j, factors[0], 0.0)
            for i in range(j + 1, 8):
                entry = splat_row(cols[i][0], j)
                cols[i] = [c - f * entry for c, f in zip(cols[i], factors)]
            for t in range(s, n):
                strips[t] = strips[t] - factors[t - s] * row
        scaled.append(done)
    return jnp.concatenate(scaled, 0)[:, R:]


def factor_kernel(far_ref, p_ref, q_ref, p_round_ref):
    both = far_ref[0] + far_ref[1] + (far_ref[2] + far_ref[3])
    inverse = inverse_factor(unpack(both[32:]))
    q_half = dot(inverse, unpack(both[:32]), ((1,), (0,)), precision=HIGH) * (1.0 / DP)
    q_ref[...] = jnp.broadcast_to(pack(q_half).astype(BF16)[None], q_ref.shape)
    p_round_ref[...] = dot(p_ref[...], inverse, ((1,), (1,)), precision=HIGH).astype(BF16)


def update_kernel(q_ref, p_ref, blocks_ref, update_ref, error_ref, q_new_ref):
    n = q_ref.shape[1]

    def columns(i):
        even, odd = q_ref[0, i].astype(F32), q_ref[1, i].astype(F32)
        return (
            jnp.concatenate([even[:, :R], odd[:, :R]], 1),
            jnp.concatenate([even[:, R:], odd[:, R:]], 1),
        )

    for k in range(n // CORES):
        pieces = [jnp.concatenate(columns(CORES * k + c), 0) for c in range(CORES)]
        q = jnp.concatenate(pieces, 1).astype(BF16)
        full = dot(p_ref[...], q, ((1,), (0,)))
        span = slice(COLS * k, COLS * (k + 1))
        update_ref[:, span] = full.astype(BF16)
        for c in range(CORES):
            rows = slice(HALF * c, HALF * (c + 1))
            error_ref[0, rows, span] = (blocks_ref[CORES * k + c].astype(F32) - full[rows]).astype(BF16)

    z = lax.axis_index("tensor")
    step = pl.program_id(0)

    @pl.when(step == lax.div(z, n // CORES))
    def _():
        for c in range(CORES):
            upper, lower = columns(CORES * lax.rem(z, n // CORES) + c)
            q_new_ref[:32, 128 * c : 128 * (c + 1)] = upper
            q_new_ref[32:, 128 * c : 128 * (c + 1)] = lower


STEPS = 4


def body(grad, error, q_start):
    wide = pl.BlockSpec((1, ROWS, D // STEPS), lambda j: (0, 0, j))
    tall = pl.BlockSpec((DP // STEPS, HALF, COLS), lambda j: (j, 0, 0))
    factor_t = lax.ppermute(q_start.T, ("dp", "tensor"), factor_route())
    own = pl.pallas_call(
        correct_kernel,
        grid=(STEPS,),
        in_specs=[wide, wide],
        out_specs=tall,
        out_shape=shape(DP, HALF, COLS, dtype=BF16),
    )(grad, error)
    blocks = lax.all_to_all(own, "dp", 0, 0)
    total, part = pl.pallas_call(
        sketch_kernel, out_shape=(shape(HALF, COLS), shape(CHIPS, 32, 128))
    )(blocks, factor_t)
    part = lax.all_to_all(part, "dp", 0, 0, axis_index_groups=PLANE)
    give, keep = pl.pallas_call(basis_kernel, out_shape=(shape(128, 128), shape(128, 128)))(part, total)
    got = lax.ppermute(give, "dp", SWAP)
    near, p_sum = pl.pallas_call(near_kernel, out_shape=(shape(4, 64, 128), shape(ROWS, R)))(keep, got)
    near = lax.all_to_all(near, "tensor", 0, 0, axis_index_groups=NEAR)
    far = pl.pallas_call(far_kernel, out_shape=shape(4, 64, 128))(near)
    far = lax.all_to_all(far, "tensor", 0, 0, axis_index_groups=FAR)
    q_blocks, p_round = pl.pallas_call(
        factor_kernel,
        out_shape=(shape(2 * DP, 32, 128, dtype=BF16), shape(ROWS, R, dtype=BF16)),
    )(far, p_sum)
    q_blocks = lax.all_to_all(q_blocks, ("dp", "tensor"), 0, 0, axis_index_groups=PAIRED)
    update, new_error, q_mine = pl.pallas_call(
        update_kernel,
        grid=(STEPS,),
        in_specs=[
            pl.BlockSpec((2, DP // STEPS, 32, 128), lambda j: (0, j, 0, 0)),
            pl.BlockSpec((ROWS, R), lambda j: (0, 0)),
            tall,
        ],
        out_specs=[
            pl.BlockSpec((ROWS, D // STEPS), lambda j: (0, j)),
            wide,
            pl.BlockSpec((R, COLS), lambda j: (0, 0)),
        ],
        out_shape=(shape(ROWS, D, dtype=BF16), shape(1, ROWS, D, dtype=BF16), shape(R, COLS)),
    )(q_blocks.reshape(2, DP, 32, 128), p_round, own)
    return (update, new_error, q_mine.T)


def solution(mesh):
    placed = (P("dp", "tensor", None), P("dp", "tensor", None), P("tensor", None))
    return jax.shard_map(
        body,
        mesh=mesh,
        in_specs=placed,
        out_specs=(P("tensor", None), P("dp", "tensor", None), P("tensor", None)),
        check_vma=False,
    )
```

time: 114 us -> 123 us (1.079)
  blocking collectives: 8.57 us -> 64.4 us
  waiting for transfers between devices: 37.3 us -> 6.83 us
  starting transfers between devices: 52.3 us -> 28.4 us
  Pallas kernels: 4.39 us -> 20 us
  other arithmetic: 3.48 us -> 0 us
  matrix products: 2.39 us -> 0 us
  local copies, waits for them, and re-layouts: 3.85 us -> 2.21 us
    all_to_all x1 -> x4, blocking collectives: 8.57 us -> 64.4 us  [the longest x1 22.1 us: body(): far = lax.all_to_all(far, 'tensor', 0, 0, axis_index_groups=FAR)]
    all_to_all x4 -> x1, waiting for transfers between devices: 35.4 us -> 0.01 us  [body(): blocks = lax.all_to_all(own, 'dp', 0, 0)]
    all_to_all x4 -> x1, starting transfers between devices: 34.6 us -> 10.6 us  [body(): blocks = lax.all_to_all(own, 'dp', 0, 0)]
    pallas_call x1 -> x7, Pallas kernels: 4.39 us -> 20 us  [the longest x1 4.42 us: body(): pl.pallas_call(factor_kernel, out_shape=(shape(2 * DP, 32, 128, dtype=BF1...]
    ppermute x1, waiting for transfers between devices: 1 us -> 5.74 us  [body(): factor_t = lax.ppermute(q_start.T, ('dp', 'tensor'), factor_route())]
    convert_element_type x2 -> x0, other arithmetic: 2.42 us -> none  [the longest x1 1.79 us: body(): (grad[0].astype(jnp.float32) + error[0].astype(jnp.float32)).astype(jnp.b...]
    dot_general x4 -> x0, matrix products: 2.39 us -> none  [the longest x1 1.73 us: body(): full_update = jnp.dot(p_round, q_round, preferred_element_type=jnp.float32)]
    broadcast_in_dim x3 -> x0, local copies, waits for them, and re-layouts: 1.44 us -> none  [share(): jnp.broadcast_to(x[None], (size,) + x.shape)]
  transfers between devices with their start and end apart: 6 -> 3, of which waited for: 6 -> 2; matrix products, arithmetic and copies ran while one was open for 1% -> 0% of each run, Pallas kernels for 0% -> 0%
where the time goes in v3:
time: 123 us; the launch traced here: 122 us
  blocking collectives  64.4 us (52%)
  starting transfers between devices  28.4 us (23%)
  Pallas kernels  20 us (16%)
  waiting for transfers between devices  6.83 us (6%)
  local copies, waits for them, and re-layouts  2.21 us (2%)
    all_to_all x1, blocking collectives, body(): far = lax.all_to_all(far, 'tensor', 0, 0, axis_index_groups=FAR)  22.1 us
    all_to_all x1, blocking collectives, body(): lax.all_to_all(q_blocks, ('dp', 'tensor'), 0, 0, axis_index_groups=PAIRED)  21.8 us
    ppermute x1, starting transfers between devices, body(): factor_t = lax.ppermute(q_start.T, ('dp', 'tensor'), factor_route())  13.6 us
    all_to_all x1, blocking collectives, body(): part = lax.all_to_all(part, 'dp', 0, 0, axis_index_groups=PLANE)  11.6 us
    all_to_all x1, starting transfers between devices, body(): blocks = lax.all_to_all(own, 'dp', 0, 0)  10.6 us
    all_to_all x1, blocking collectives, body(): near = lax.all_to_all(near, 'tensor', 0, 0, axis_index_groups=NEAR)  8.89 us
    ppermute x1, waiting for transfers between devices, body(): factor_t = lax.ppermute(q_start.T, ('dp', 'tensor'), factor_route())  5.74 us
    pallas_call x1, Pallas kernels, body(): pl.pallas_call(factor_kernel, out_shape=(shape(2 * DP, 32, 128, dtype=BF1...  4.42 us
  transfers between devices with their start and end apart: 3, of which 2 were waited for; matrix products, arithmetic and copies ran while one was open for 0% of the time, Pallas kernels for 0%

profile of v3, /device:TPU:1, one launch (start us, length us, event | category | flops | bytes accessed | tf_op | source)
XLA Modules:
  0.0 122.4 jit_solution(3346897389052996019)
XLA Ops:
  0.6 3.7 %shard_map.58.blocks_ref = bf16[32,64,256]{2,1,0:T(8,128)(2,1)} custom-call(bf16[1,128,4096]{2,1,0:T(8,128)(2,1)} %grad_ref.1, bf16[1,128,4096]{2,1,0:T(8,128)(2,1)} %error_ref.1), custom_call_target="tpu_custom_call" | custom-call | tf_op jit(solution)/shard_map/pallas_call | solution.py:193
  4.3 0.0 copy-start.3
  4.3 10.6 %all-to-all-start = ((bf16[32,64,256]{2,1,0:T(8,128)(2,1)}), bf16[32,64,256]{2,1,0:T(8,128)(2,1)S(1)}, u32[]{:S(2)}, u32[]{:S(2)}) async-start(bf16[32,64,256]{2,1,0:T(8,128)(2,1)} %shard_map.58.blocks_ref), calls=%async_computation | async-start | bytes 2097152 | tf_op jit(solution)/shard_map/all_to_all | solution.py:200
  14.9 0.0 copy-done.3
  14.9 13.6 %collective-permute-start = (bf16[64,256]{1,0:T(8,128)(2,1)S(1)}, bf16[64,256]{1,0:T(8,128)(2,1)S(1)}, u32[]{:S(2)}, u32[]{:S(2)}) collective-permute-start(bf16[64,256]{1,0:T(8,128)(2,1)S(1)} %bitcast.5), channel_id=1, source_target_pairs={{0,8},{16,24},{32,7},{48,23},{96,9},{112,25},{128,6},{144,22},{384... | collective-permute-start | bytes 98312 | tf_op jit(solution)/shard_map/ppermute | solution.py:192
  28.5 5.7 %collective-permute-done.factor_ref = bf16[64,256]{1,0:T(8,128)(2,1)S(1)} collective-permute-done((bf16[64,256]{1,0:T(8,128)(2,1)S(1)}, bf16[64,256]{1,0:T(8,128)(2,1)S(1)}, u32[]{:S(2)}, u32[]{:S(2)}) %collective-permute-start) | collective-permute-done | bytes 32800 | tf_op jit(solution)/shard_map/ppermute | solution.py:192
  34.2 0.0 copy-start.2
  34.2 0.0 all-to-all-done.blocks_ref
  34.2 0.6 copy-done.2
  34.8 0.0 copy-start
  34.8 1.0 copy-done
  35.8 2.4 %shard_map.59 = (f32[64,256]{1,0:T(8,128)}, f32[16,32,128]{2,1,0:T(8,128)}) custom-call(bf16[32,64,256]{2,1,0:T(8,128)(2,1)} %copy-done, bf16[64,256]{1,0:T(8,128)(2,1)} %copy-done.2), custom_call_target="tpu_custom_call" | custom-call | tf_op jit(solution)/shard_map/pallas_call | solution.py:201
  38.2 11.6 %all_to_all.25.share_ref = f32[16,32,128]{2,1,0:T(8,128)} all-to-all(f32[16,32,128]{2,1,0:T(8,128)} %get-tuple-element.14), channel_id=1, replica_groups={{0,32,64,96,128,160,192,224,256,288,320,352,384,416,448,480},{16,48,80,..., dimensions={0} | all-to-all | bytes 524288 | tf_op jit(solution)/shard_map/all_to_all | solution.py:204
  49.7 2.0 %shard_map.60 = (f32[128,128]{1,0:T(8,128)}, f32[128,128]{1,0:T(8,128)}) custom-call(f32[16,32,128]{2,1,0:T(8,128)} %all_to_all.25.share_ref, f32[64,256]{1,0:T(8,128)} %get-tuple-element.15.total_ref), custom_call_target="tpu_custom_call" | custom-call | tf_op jit(solution)/shard_map/pallas_call | solution.py:205
  51.7 4.2 %collective-permute-start.1 = (f32[128,128]{1,0:T(8,128)}, f32[128,128]{1,0:T(8,128)S(1)}, u32[]{:S(2)}, u32[]{:S(2)}) collective-permute-start(f32[128,128]{1,0:T(8,128)} %get-tuple-element.17), channel_id=1, source_target_pairs={{0,16},{16,0},{32,48},{48,32},{64,80},{80,64},{96,112},{112,96},{1... | collective-permute-start | bytes 196616 | tf_op jit(solution)/shard_map/ppermute | solution.py:206
  55.9 1.1 collective-permute-done.1.got_ref
  57.0 0.0 copy-start.1
  57.0 0.6 copy-done.1
  57.7 1.6 %shard_map.61 = (f32[4,64,128]{2,1,0:T(8,128)}, f32[128,64]{1,0:T(8,128)}) custom-call(f32[128,128]{1,0:T(8,128)} %get-tuple-element.16.keep_ref, f32[128,128]{1,0:T(8,128)} %copy-done.1), custom_call_target="tpu_custom_call" | custom-call | tf_op jit(solution)/shard_map/pallas_call | solution.py:207
  59.3 8.9 %all_to_all.26.near_ref = f32[4,64,128]{2,1,0:T(8,128)} all-to-all(f32[4,64,128]{2,1,0:T(8,128)} %get-tuple-element.18), channel_id=1, replica_groups={{0,1,2,3},{4,5,6,7},{8,9,10,11},{12,13,14,15},{16,17,18,19},{20,21,22,2..., dimensions={0} | all-to-all | bytes 262144 | tf_op jit(solution)/shard_map/all_to_all | solution.py:208
  68.2 1.6 %shard_map.62 = f32[4,64,128]{2,1,0:T(8,128)} custom-call(f32[4,64,128]{2,1,0:T(8,128)} %all_to_all.26.near_ref), custom_call_target="tpu_custom_call" | custom-call | tf_op jit(solution)/shard_map/pallas_call | solution.py:209
  69.7 22.1 %all_to_all.27.far_ref = f32[4,64,128]{2,1,0:T(8,128)} all-to-all(f32[4,64,128]{2,1,0:T(8,128)} %shard_map.62), channel_id=1, replica_groups={{0,4,8,12},{1,5,9,13},{2,6,10,14},{3,7,11,15},{16,20,24,28},{17,21,25,2..., dimensions={0} | all-to-all | bytes 262144 | tf_op jit(solution)/shard_map/all_to_all | solution.py:210
  91.9 4.4 %shard_map.63 = (bf16[64,32,128]{2,1,0:T(8,128)(2,1)}, bf16[128,64]{1,0:T(8,128)(2,1)}) custom-call(f32[4,64,128]{2,1,0:T(8,128)} %all_to_all.27.far_ref, f32[128,64]{1,0:T(8,128)} %get-tuple-element.19.p_ref), custom_call_target="tpu_custom_call" | custom-call | tf_op jit(solution)/shard_map/pallas_call | solution.py:211
  96.3 21.8 %all_to_all.28 = bf16[64,32,128]{2,1,0:T(8,128)(2,1)} all-to-all(bf16[64,32,128]{2,1,0:T(8,128)(2,1)} %get-tuple-element.20), channel_id=1, replica_groups={{0,16,32,48,64,80,96,112,128,144,160,176,192,208,224,240,256,272,288,30..., dimensions={0} | all-to-all | bytes 1048576 | tf_op jit(solution)/shard_map/all_to_all | solution.py:215
  118.1 4.3 %shard_map.64 = (bf16[128,4096]{1,0:T(8,128)(2,1)}, bf16[1,128,4096]{2,1,0:T(8,128)(2,1)}, f32[64,256]{1,0:T(8,128)}) custom-call(bf16[2,32,32,128]{3,2,1,0:T(8,128)(2,1)} %bitcast.3, bf16[128,64]{1,0:T(8,128)(2,1)} %get-tuple-element.21.p_ref, bf16[32,64,256]{2,1,0:T(8,128)(2,1)} %shard_map.58.blocks_ref), custom_call_target="tpu_custom_call" | custom-call | tf_op jit(solution)/shard_map/pallas_call | solution.py:216
Async XLA Ops:
  4.3 10.6 %copy-start.3 = (bf16[256,64]{0,1:T(8,128)(2,1)S(1)}, bf16[256,64]{0,1:T(8,128)(2,1)}, u32[]{:S(2)}) copy-start(bf16[256,64]{0,1:T(8,128)(2,1)} %param.5) | copy-start | bytes 98308
  4.3 29.9 %all-to-all-start = ((bf16[32,64,256]{2,1,0:T(8,128)(2,1)}), bf16[32,64,256]{2,1,0:T(8,128)(2,1)S(1)}, u32[]{:S(2)}, u32[]{:S(2)}) async-start(bf16[32,64,256]{2,1,0:T(8,128)(2,1)} %shard_map.58.blocks_ref), calls=%async_computation | async-start | bytes 2097152 | tf_op jit(solution)/shard_map/all_to_all | solution.py:200
  14.9 19.3 %collective-permute-start = (bf16[64,256]{1,0:T(8,128)(2,1)S(1)}, bf16[64,256]{1,0:T(8,128)(2,1)S(1)}, u32[]{:S(2)}, u32[]{:S(2)}) collective-permute-start(bf16[64,256]{1,0:T(8,128)(2,1)S(1)} %bitcast.5), channel_id=1, source_target_pairs={{0,8},{16,24},{32,7},{48,23},{96,9},{112,25},{128,6},{144,22},{384... | collective-permute-start | bytes 98312 | tf_op jit(solution)/shard_map/ppermute | solution.py:192
  34.2 0.6 copy-start.2
  34.8 1.0 copy-start
  51.7 5.3 %collective-permute-start.1 = (f32[128,128]{1,0:T(8,128)}, f32[128,128]{1,0:T(8,128)S(1)}, u32[]{:S(2)}, u32[]{:S(2)}) collective-permute-start(f32[128,128]{1,0:T(8,128)} %get-tuple-element.17), channel_id=1, source_target_pairs={{0,16},{16,0},{32,48},{48,32},{64,80},{80,64},{96,112},{112,96},{1... | collective-permute-start | bytes 196616 | tf_op jit(solution)/shard_map/ppermute | solution.py:206
  57.0 0.6 copy-start.1

commit v4 on v3

--- a/solution.py
+++ b/solution.py
@@ -15,6 +15,7 @@
 D = 4096
 COLS = D // CHIPS
 R = 64
+PARTS = 4
 HIGH = lax.Precision.HIGHEST
 F32, BF16 = jnp.float32, jnp.bfloat16
 
@@ -22,7 +23,6 @@
 NEAR = [[4 * a + b for b in range(4)] for a in range(4)]
 FAR = [[4 * a + b for a in range(4)] for b in range(4)]
 SWAP = [(i, i ^ 1) for i in range(DP)]
-PAIRED = [[i * DEPTH + 2 * a + b for b in range(2) for i in range(DP)] for a in range(DEPTH // 2)]
 
 
 def ring(a, b, n):
@@ -59,11 +59,10 @@
     return lax.dot_general(a, b, (over, ((), ())), preferred_element_type=F32, **kw)
 
 
-def correct_kernel(grad_ref, error_ref, out_ref):
-    x = (grad_ref[0].astype(F32) + error_ref[0].astype(F32)).astype(BF16)
-    for k in range(out_ref.shape[0] // CORES):
+def block_kernel(rows_ref, out_ref):
+    for k in range(CHIPS):
         for c in range(CORES):
-            out_ref[CORES * k + c] = x[HALF * c : HALF * (c + 1), COLS * k : COLS * (k + 1)]
+            out_ref[CORES * k + c] = rows_ref[HALF * c : HALF * (c + 1), COLS * k : COLS * (k + 1)]
 
 
 def sketch_kernel(blocks_ref, factor_ref, total_ref, share_ref):
@@ -92,13 +91,8 @@
 
 
 def near_kernel(keep_ref, got_ref, share_ref, p_ref):
-    both = keep_ref[:R] + got_ref[:R]
-    gram = keep_ref[R : R + 32] + got_ref[R : R + 32]
-    for half in range(2):
-        part = pack(both[:, R * half : R * (half + 1)])
-        for m in (half, half + 2):
-            share_ref[m, :32] = part
-            share_ref[m, 32:] = gram
+    both = keep_ref[: R + 32] + got_ref[: R + 32]
+    share_ref[...] = jnp.broadcast_to(both[None], share_ref.shape)
     first = lax.rem(lax.axis_index("dp"), CORES) == 0
     mine, other = unpack(keep_ref[R + 32 :]), unpack(got_ref[R + 32 :])
     p_ref[:HALF] = jnp.where(first, mine, other)
@@ -146,88 +140,84 @@
 
 def factor_kernel(far_ref, p_ref, q_ref, p_round_ref):
     both = far_ref[0] + far_ref[1] + (far_ref[2] + far_ref[3])
-    inverse = inverse_factor(unpack(both[32:]))
-    q_half = dot(inverse, unpack(both[:32]), ((1,), (0,)), precision=HIGH) * (1.0 / DP)
-    q_ref[...] = jnp.broadcast_to(pack(q_half).astype(BF16)[None], q_ref.shape)
+    inverse = inverse_factor(unpack(both[R:]))
+    q = (dot(inverse, both[:R], ((1,), (0,)), precision=HIGH) * (1.0 / DP)).astype(BF16)
+    q_ref[...] = jnp.broadcast_to(q[None], q_ref.shape)
     p_round_ref[...] = dot(p_ref[...], inverse, ((1,), (1,)), precision=HIGH).astype(BF16)
 
 
-def update_kernel(q_ref, p_ref, blocks_ref, update_ref, error_ref, q_new_ref):
-    n = q_ref.shape[1]
-
-    def columns(i):
-        even, odd = q_ref[0, i].astype(F32), q_ref[1, i].astype(F32)
-        return (
-            jnp.concatenate([even[:, :R], odd[:, :R]], 1),
-            jnp.concatenate([even[:, R:], odd[:, R:]], 1),
-        )
-
-    for k in range(n // CORES):
-        pieces = [jnp.concatenate(columns(CORES * k + c), 0) for c in range(CORES)]
-        q = jnp.concatenate(pieces, 1).astype(BF16)
-        full = dot(p_ref[...], q, ((1,), (0,)))
-        span = slice(COLS * k, COLS * (k + 1))
-        update_ref[:, span] = full.astype(BF16)
-        for c in range(CORES):
-            rows = slice(HALF * c, HALF * (c + 1))
-            error_ref[0, rows, span] = (blocks_ref[CORES * k + c].astype(F32) - full[rows]).astype(BF16)
-
+def update_kernel(
+    q_ref, p_ref, rows_ref, update_ref, error_ref, q_new_ref, update_out, error_out, q_new_out, sems, q_sem
+):
+    width = D // PARTS
     z = lax.axis_index("tensor")
-    step = pl.program_id(0)
-
-    @pl.when(step == lax.div(z, n // CORES))
-    def _():
-        for c in range(CORES):
-            upper, lower = columns(CORES * lax.rem(z, n // CORES) + c)
-            q_new_ref[:32, 128 * c : 128 * (c + 1)] = upper
-            q_new_ref[32:, 128 * c : 128 * (c + 1)] = lower
-
-
-STEPS = 4
+    for c in range(CORES):
+        q_new_out[:, 128 * c : 128 * (c + 1)] = q_ref[CORES * z + c].astype(F32)
+    q_copy = pltpu.make_async_copy(q_new_out, q_new_ref, q_sem)
+    q_copy.start()
+
+    def copies(n):
+        span = pl.ds(n * width, width)
+        return [
+            pltpu.make_async_copy(update_out.at[:, span], update_ref.at[:, span], sems.at[0, n]),
+            pltpu.make_async_copy(error_out.at[:, span], error_ref.at[0, :, span], sems.at[1, n]),
+        ]
+
+    for n in range(PARTS):
+        for k in range(n * width // COLS, (n + 1) * width // COLS):
+            q = jnp.concatenate([q_ref[CORES * k + c] for c in range(CORES)], 1)
+            full = dot(p_ref[...], q, ((1,), (0,)))
+            span = slice(COLS * k, COLS * (k + 1))
+            update_out[:, span] = full.astype(BF16)
+            error_out[:, span] = (rows_ref[:, span].astype(F32) - full).astype(BF16)
+        for copy in copies(n):
+            copy.start()
+    for n in range(PARTS):
+        for copy in copies(n):
+            copy.wait()
+    q_copy.wait()
+
+
+def kernel_call(kernel, mib=4, **kw):
+    return pl.pallas_call(
+        kernel, compiler_params=pltpu.CompilerParams(vmem_limit_bytes=mib << 20), **kw
+    )
 
 
 def body(grad, error, q_start):
-    wide = pl.BlockSpec((1, ROWS, D // STEPS), lambda j: (0, 0, j))
-    tall = pl.BlockSpec((DP // STEPS, HALF, COLS), lambda j: (j, 0, 0))
+    vmem, hbm = pl.BlockSpec(memory_space=pltpu.VMEM), pl.BlockSpec(memory_space=pltpu.HBM)
     factor_t = lax.ppermute(q_start.T, ("dp", "tensor"), factor_route())
-    own = pl.pallas_call(
-        correct_kernel,
-        grid=(STEPS,),
-        in_specs=[wide, wide],
-        out_specs=tall,
-        out_shape=shape(DP, HALF, COLS, dtype=BF16),
-    )(grad, error)
-    blocks = lax.all_to_all(own, "dp", 0, 0)
-    total, part = pl.pallas_call(
+    corrected = (grad[0].astype(F32) + error[0].astype(F32)).astype(BF16)
+    blocks = kernel_call(block_kernel, out_shape=shape(DP, HALF, COLS, dtype=BF16))(corrected)
+    blocks = lax.all_to_all(blocks, "dp", 0, 0)
+    total, part = kernel_call(
         sketch_kernel, out_shape=(shape(HALF, COLS), shape(CHIPS, 32, 128))
     )(blocks, factor_t)
     part = lax.all_to_all(part, "dp", 0, 0, axis_index_groups=PLANE)
-    give, keep = pl.pallas_call(basis_kernel, out_shape=(shape(128, 128), shape(128, 128)))(part, total)
+    give, keep = kernel_call(basis_kernel, out_shape=(shape(128, 128), shape(128, 128)))(part, total)
     got = lax.ppermute(give, "dp", SWAP)
-    near, p_sum = pl.pallas_call(near_kernel, out_shape=(shape(4, 64, 128), shape(ROWS, R)))(keep, got)
+    near, p_sum = kernel_call(near_kernel, out_shape=(shape(4, R + 32, 128), shape(ROWS, R)))(keep, got)
     near = lax.all_to_all(near, "tensor", 0, 0, axis_index_groups=NEAR)
-    far = pl.pallas_call(far_kernel, out_shape=shape(4, 64, 128))(near)
+    far = kernel_call(far_kernel, out_shape=shape(4, R + 32, 128))(near)
     far = lax.all_to_all(far, "tensor", 0, 0, axis_index_groups=FAR)
-    q_blocks, p_round = pl.pallas_call(
+    q_blocks, p_round = kernel_call(
         factor_kernel,
-        out_shape=(shape(2 * DP, 32, 128, dtype=BF16), shape(ROWS, R, dtype=BF16)),
+        out_shape=(shape(DP, R, 128, dtype=BF16), shape(ROWS, R, dtype=BF16)),
     )(far, p_sum)
-    q_blocks = lax.all_to_all(q_blocks, ("dp", "tensor"), 0, 0, axis_index_groups=PAIRED)
-    update, new_error, q_mine = pl.pallas_call(
+    q_blocks = lax.all_to_all(q_blocks, "dp", 0, 0)
+    update, new_error, q_mine = kernel_call(
         update_kernel,
-        grid=(STEPS,),
-        in_specs=[
-            pl.BlockSpec((2, DP // STEPS, 32, 128), lambda j: (0, j, 0, 0)),
-            pl.BlockSpec((ROWS, R), lambda j: (0, 0)),
-            tall,
+        in_specs=[vmem, vmem, vmem],
+        out_specs=[hbm, hbm, hbm],
+        out_shape=(shape(ROWS, D, dtype=BF16), shape(1, ROWS, D, dtype=BF16), shape(R, COLS)),
+        scratch_shapes=[
+            pltpu.VMEM((ROWS, D), BF16),
+            pltpu.VMEM((ROWS, D), BF16),
+            pltpu.VMEM((R, COLS), F32),
+            pltpu.SemaphoreType.DMA((2, PARTS)),
+            pltpu.SemaphoreType.DMA,
         ],
-        out_specs=[
-            pl.BlockSpec((ROWS, D // STEPS), lambda j: (0, j)),
-            wide,
-            pl.BlockSpec((R, COLS), lambda j: (0, 0)),
-        ],
-        out_shape=(shape(ROWS, D, dtype=BF16), shape(1, ROWS, D, dtype=BF16), shape(R, COLS)),
-    )(q_blocks.reshape(2, DP, 32, 128), p_round, own)
+    )(q_blocks, p_round, corrected)
     return (update, new_error, q_mine.T)
 
 

time: 123 us -> 108 us (0.88)
  Pallas kernels: 20 us -> 6.26 us
  local copies, waits for them, and re-layouts: 2.21 us -> 0.01 us
  other arithmetic: 0 us -> 1.79 us
    pallas_call x7, Pallas kernels: 20 us -> 6.26 us  [the longest x1 2.67 us: body(): kernel_call(factor_kernel, out_shape=(shape(DP, R, 128, dtype=BF16), shap...]
    all_to_all x1, blocking collectives: 22.1 us -> 26 us  [body(): far = lax.all_to_all(far, 'tensor', 0, 0, axis_index_groups=FAR)]
    all_to_all x1, blocking collectives: 21.8 us -> 19.2 us  [body(): q_blocks = lax.all_to_all(q_blocks, 'dp', 0, 0)]
    unnamed x8 -> x2, local copies, waits for them, and re-layouts: 2.21 us -> 0.01 us
    convert_element_type x0 -> x1, other arithmetic: none -> 1.79 us  [body(): corrected = (grad[0].astype(F32) + error[0].astype(F32)).astype(BF16)]
    all_to_all x1, blocking collectives: 11.6 us -> 9.96 us  [body(): part = lax.all_to_all(part, 'dp', 0, 0, axis_index_groups=PLANE)]
where the time goes in v4:
time: 108 us; the launch traced here: 107 us
  blocking collectives  63.7 us (59%)
  starting transfers between devices  28.4 us (26%)
  waiting for transfers between devices  6.63 us (6%)
  Pallas kernels  6.26 us (6%)
  other arithmetic  1.79 us (2%)
    all_to_all x1, blocking collectives, body(): far = lax.all_to_all(far, 'tensor', 0, 0, axis_index_groups=FAR)  26 us
    all_to_all x1, blocking collectives, body(): q_blocks = lax.all_to_all(q_blocks, 'dp', 0, 0)  19.2 us
    ppermute x1, starting transfers between devices, body(): factor_t = lax.ppermute(q_start.T, ('dp', 'tensor'), factor_route())  13.6 us
    all_to_all x1, starting transfers between devices, body(): blocks = lax.all_to_all(blocks, 'dp', 0, 0)  10.6 us
    all_to_all x1, blocking collectives, body(): part = lax.all_to_all(part, 'dp', 0, 0, axis_index_groups=PLANE)  9.96 us
    all_to_all x1, blocking collectives, body(): near = lax.all_to_all(near, 'tensor', 0, 0, axis_index_groups=NEAR)  8.58 us
    ppermute x1, waiting for transfers between devices, body(): factor_t = lax.ppermute(q_start.T, ('dp', 'tensor'), factor_route())  5.74 us
    ppermute x1, starting transfers between devices, body(): got = lax.ppermute(give, 'dp', SWAP)  4.2 us
  transfers between devices with their start and end apart: 3, of which 2 were waited for; matrix products, arithmetic and copies ran while one was open for 0% of the time, Pallas kernels for 0%

profile of v4, /device:TPU:1, one launch (start us, length us, event | category | flops | bytes accessed | tf_op | source)
XLA Modules:
  0.0 107.5 jit_solution(16190784132324311368)
XLA Ops:
  0.6 1.8 %fusion.rows_ref = bf16[128,4096]{1,0:T(8,128)(2,1)S(1)} fusion(bf16[1,128,4096]{2,1,0:T(8,128)(2,1)} %param.4, bf16[1,128,4096]{2,1,0:T(8,128)(2,1)} %param.3), kind=kLoop, calls=%fused_computation.1 | loop fusion | flops 2097152 | bytes 3145728 | tf_op jit(solution)/shard_map/convert_element_type | solution.py:190
  2.4 1.0 shard_map.58
  3.5 0.0 copy-start
  3.5 10.6 %all-to-all-start = ((bf16[32,64,256]{2,1,0:T(8,128)(2,1)}), bf16[32,64,256]{2,1,0:T(8,128)(2,1)S(1)}, u32[]{:S(2)}, u32[]{:S(2)}) async-start(bf16[32,64,256]{2,1,0:T(8,128)(2,1)} %shard_map.58), calls=%async_computation | async-start | bytes 2097152 | tf_op jit(solution)/shard_map/all_to_all | solution.py:192
  14.1 0.0 copy-done
  14.1 13.6 %collective-permute-start = (bf16[64,256]{1,0:T(8,128)(2,1)S(1)}, bf16[64,256]{1,0:T(8,128)(2,1)S(1)}, u32[]{:S(2)}, u32[]{:S(2)}) collective-permute-start(bf16[64,256]{1,0:T(8,128)(2,1)S(1)} %bitcast.5), channel_id=1, source_target_pairs={{0,8},{16,24},{32,7},{48,23},{96,9},{112,25},{128,6},{144,22},{384... | collective-permute-start | bytes 98312 | tf_op jit(solution)/shard_map/ppermute | solution.py:189
  27.7 5.7 %collective-permute-done.factor_ref = bf16[64,256]{1,0:T(8,128)(2,1)S(1)} collective-permute-done((bf16[64,256]{1,0:T(8,128)(2,1)S(1)}, bf16[64,256]{1,0:T(8,128)(2,1)S(1)}, u32[]{:S(2)}, u32[]{:S(2)}) %collective-permute-start) | collective-permute-done | bytes 32800 | tf_op jit(solution)/shard_map/ppermute | solution.py:189
  33.4 0.0 all-to-all-done.blocks_ref
  33.4 0.4 shard_map.59
  33.8 10.0 %all_to_all.25.share_ref = f32[16,32,128]{2,1,0:T(8,128)S(1)} all-to-all(f32[16,32,128]{2,1,0:T(8,128)S(1)} %get-tuple-element.14), channel_id=1, replica_groups={{0,32,64,96,128,160,192,224,256,288,320,352,384,416,448,480},{16,48,80,..., dimensions={0} | all-to-all | bytes 524288 | tf_op jit(solution)/shard_map/all_to_all | solution.py:196
  43.8 0.4 shard_map.60
  44.2 4.2 %collective-permute-start.1 = (f32[128,128]{1,0:T(8,128)S(1)}, f32[128,128]{1,0:T(8,128)S(1)}, u32[]{:S(2)}, u32[]{:S(2)}) collective-permute-start(f32[128,128]{1,0:T(8,128)S(1)} %get-tuple-element.17), channel_id=1, source_target_pairs={{0,16},{16,0},{32,48},{48,32},{64,80},{80,64},{96,112},{112,96},{1... | collective-permute-start | bytes 196616 | tf_op jit(solution)/shard_map/ppermute | solution.py:198
  48.4 0.9 collective-permute-done.1.got_ref
  49.3 0.1 shard_map.61
  49.4 8.6 %all_to_all.26.near_ref = f32[4,96,128]{2,1,0:T(8,128)S(1)} all-to-all(f32[4,96,128]{2,1,0:T(8,128)S(1)} %get-tuple-element.18), channel_id=1, replica_groups={{0,1,2,3},{4,5,6,7},{8,9,10,11},{12,13,14,15},{16,17,18,19},{20,21,22,2..., dimensions={0} | all-to-all | bytes 393216 | tf_op jit(solution)/shard_map/all_to_all | solution.py:200
  58.0 26.0 %all_to_all.27.far_ref = f32[4,96,128]{2,1,0:T(8,128)S(1)} all-to-all(f32[4,96,128]{2,1,0:T(8,128)S(1)} %shard_map.62), channel_id=1, replica_groups={{0,4,8,12},{1,5,9,13},{2,6,10,14},{3,7,11,15},{16,20,24,28},{17,21,25,2..., dimensions={0} | all-to-all | bytes 393216 | tf_op jit(solution)/shard_map/all_to_all | solution.py:202
  84.0 2.7 %shard_map.63 = (bf16[32,64,128]{2,1,0:T(8,128)(2,1)S(1)}, bf16[128,64]{1,0:T(8,128)(2,1)S(1)}) custom-call(f32[4,96,128]{2,1,0:T(8,128)S(1)} %all_to_all.27.far_ref, f32[128,64]{1,0:T(8,128)S(1)} %get-tuple-element.19.p_ref), custom_call_target="tpu_custom_call" | custom-call | tf_op jit(solution)/shard_map/pallas_call | solution.py:203
  86.6 19.2 %all_to_all.28.q_ref = bf16[32,64,128]{2,1,0:T(8,128)(2,1)S(1)} all-to-all(bf16[32,64,128]{2,1,0:T(8,128)(2,1)S(1)} %get-tuple-element.20), channel_id=1, replica_groups=mesh['dp'=32,'tensor'=16] {'dp'}, dimensions={0} | all-to-all | bytes 1048576 | tf_op jit(solution)/shard_map/all_to_all | solution.py:207
  105.8 1.6 %shard_map.64 = (bf16[128,4096]{1,0:T(8,128)(2,1)}, bf16[1,128,4096]{2,1,0:T(8,128)(2,1)}, f32[64,256]{1,0:T(8,128)}) custom-call(bf16[32,64,128]{2,1,0:T(8,128)(2,1)S(1)} %all_to_all.28.q_ref, bf16[128,64]{1,0:T(8,128)(2,1)S(1)} %get-tuple-element.21.p_ref, bf16[128,4096]{1,0:T(8,128)(2,1)S(1)} %fusion.rows_ref), custom_call_target="tpu_custom_call" | custom-call | tf_op jit(solution)/shard_map/pallas_call | solution.py:208
  (1 shorter events, 0.0 us)
Async XLA Ops:
  3.5 10.6 %copy-start = (bf16[256,64]{0,1:T(8,128)(2,1)S(1)}, bf16[256,64]{0,1:T(8,128)(2,1)}, u32[]{:S(2)}) copy-start(bf16[256,64]{0,1:T(8,128)(2,1)} %param.5) | copy-start | bytes 98308
  3.5 29.9 %all-to-all-start = ((bf16[32,64,256]{2,1,0:T(8,128)(2,1)}), bf16[32,64,256]{2,1,0:T(8,128)(2,1)S(1)}, u32[]{:S(2)}, u32[]{:S(2)}) async-start(bf16[32,64,256]{2,1,0:T(8,128)(2,1)} %shard_map.58), calls=%async_computation | async-start | bytes 2097152 | tf_op jit(solution)/shard_map/all_to_all | solution.py:192
  14.1 19.3 %collective-permute-start = (bf16[64,256]{1,0:T(8,128)(2,1)S(1)}, bf16[64,256]{1,0:T(8,128)(2,1)S(1)}, u32[]{:S(2)}, u32[]{:S(2)}) collective-permute-start(bf16[64,256]{1,0:T(8,128)(2,1)S(1)} %bitcast.5), channel_id=1, source_target_pairs={{0,8},{16,24},{32,7},{48,23},{96,9},{112,25},{128,6},{144,22},{384... | collective-permute-start | bytes 98312 | tf_op jit(solution)/shard_map/ppermute | solution.py:189
  44.2 5.1 %collective-permute-start.1 = (f32[128,128]{1,0:T(8,128)S(1)}, f32[128,128]{1,0:T(8,128)S(1)}, u32[]{:S(2)}, u32[]{:S(2)}) collective-permute-start(f32[128,128]{1,0:T(8,128)S(1)} %get-tuple-element.17), channel_id=1, source_target_pairs={{0,16},{16,0},{32,48},{48,32},{64,80},{80,64},{96,112},{112,96},{1... | collective-permute-start | bytes 196616 | tf_op jit(solution)/shard_map/ppermute | solution.py:198

commit v5 on v4

--- a/solution.py
+++ b/solution.py
@@ -100,8 +100,7 @@
 
 
 def far_kernel(near_ref, share_ref):
-    both = near_ref[0] + near_ref[1] + (near_ref[2] + near_ref[3])
-    share_ref[...] = jnp.broadcast_to(both[None], share_ref.shape)
+    share_ref[...] = near_ref[0] + near_ref[1] + (near_ref[2] + near_ref[3])
 
 
 def splat_row(x, row):
@@ -198,8 +197,8 @@
     got = lax.ppermute(give, "dp", SWAP)
     near, p_sum = kernel_call(near_kernel, out_shape=(shape(4, R + 32, 128), shape(ROWS, R)))(keep, got)
     near = lax.all_to_all(near, "tensor", 0, 0, axis_index_groups=NEAR)
-    far = kernel_call(far_kernel, out_shape=shape(4, R + 32, 128))(near)
-    far = lax.all_to_all(far, "tensor", 0, 0, axis_index_groups=FAR)
+    far = kernel_call(far_kernel, out_shape=shape(R + 32, 128))(near)
+    far = lax.all_gather(far, "tensor", axis_index_groups=FAR)
     q_blocks, p_round = kernel_call(
         factor_kernel,
         out_shape=(shape(DP, R, 128, dtype=BF16), shape(ROWS, R, dtype=BF16)),

time: 108 us -> 105 us (0.972)
  blocking collectives: 63.7 us -> 60.4 us
    all_to_all x1 -> x0, blocking collectives: 26 us -> none  [body(): far = lax.all_to_all(far, 'tensor', 0, 0, axis_index_groups=FAR)]
    all_gather x0 -> x1, blocking collectives: none -> 21.4 us  [body(): far = lax.all_gather(far, 'tensor', axis_index_groups=FAR)]
    all_to_all x1, blocking collectives: 19.2 us -> 20.5 us  [body(): q_blocks = lax.all_to_all(q_blocks, 'dp', 0, 0)]
where the time goes in v5:
time: 105 us; the launch traced here: 104 us
  blocking collectives  60.4 us (58%)
  starting transfers between devices  28.4 us (27%)
  waiting for transfers between devices  6.63 us (6%)
  Pallas kernels  6.25 us (6%)
  other arithmetic  1.79 us (2%)
    all_gather x1, blocking collectives, body(): far = lax.all_gather(far, 'tensor', axis_index_groups=FAR)  21.4 us
    all_to_all x1, blocking collectives, body(): q_blocks = lax.all_to_all(q_blocks, 'dp', 0, 0)  20.5 us
    ppermute x1, starting transfers between devices, body(): factor_t = lax.ppermute(q_start.T, ('dp', 'tensor'), factor_route())  13.6 us
    all_to_all x1, starting transfers between devices, body(): blocks = lax.all_to_all(blocks, 'dp', 0, 0)  10.6 us
    all_to_all x1, blocking collectives, body(): part = lax.all_to_all(part, 'dp', 0, 0, axis_index_groups=PLANE)  9.96 us
    all_to_all x1, blocking collectives, body(): near = lax.all_to_all(near, 'tensor', 0, 0, axis_index_groups=NEAR)  8.58 us
    ppermute x1, waiting for transfers between devices, body(): factor_t = lax.ppermute(q_start.T, ('dp', 'tensor'), factor_route())  5.74 us
    ppermute x1, starting transfers between devices, body(): got = lax.ppermute(give, 'dp', SWAP)  4.2 us
  transfers between devices with their start and end apart: 3, of which 2 were waited for; matrix products, arithmetic and copies ran while one was open for 0% of the time, Pallas kernels for 0%

profile of v5, /device:TPU:1, one launch (start us, length us, event | category | flops | bytes accessed | tf_op | source)
XLA Modules:
  0.0 104.1 jit_solution(11380867621263479605)
XLA Ops:
  0.6 1.8 %fusion.rows_ref = bf16[128,4096]{1,0:T(8,128)(2,1)S(1)} fusion(bf16[1,128,4096]{2,1,0:T(8,128)(2,1)} %param.4, bf16[1,128,4096]{2,1,0:T(8,128)(2,1)} %param.3), kind=kLoop, calls=%fused_computation.1 | loop fusion | flops 2097152 | bytes 3145728 | tf_op jit(solution)/shard_map/convert_element_type | solution.py:189
  2.4 1.0 %shard_map.58 = bf16[32,64,256]{2,1,0:T(8,128)(2,1)} custom-call(bf16[128,4096]{1,0:T(8,128)(2,1)S(1)} %fusion.rows_ref), custom_call_target="tpu_custom_call" | custom-call | tf_op jit(solution)/shard_map/pallas_call | solution.py:190
  3.5 0.0 copy-start
  3.5 10.6 %all-to-all-start = ((bf16[32,64,256]{2,1,0:T(8,128)(2,1)}), bf16[32,64,256]{2,1,0:T(8,128)(2,1)S(1)}, u32[]{:S(2)}, u32[]{:S(2)}) async-start(bf16[32,64,256]{2,1,0:T(8,128)(2,1)} %shard_map.58), calls=%async_computation | async-start | bytes 2097152 | tf_op jit(solution)/shard_map/all_to_all | solution.py:191
  14.1 0.0 copy-done
  14.1 13.6 %collective-permute-start = (bf16[64,256]{1,0:T(8,128)(2,1)S(1)}, bf16[64,256]{1,0:T(8,128)(2,1)S(1)}, u32[]{:S(2)}, u32[]{:S(2)}) collective-permute-start(bf16[64,256]{1,0:T(8,128)(2,1)S(1)} %bitcast.7), channel_id=1, source_target_pairs={{0,8},{16,24},{32,7},{48,23},{96,9},{112,25},{128,6},{144,22},{384... | collective-permute-start | bytes 98312 | tf_op jit(solution)/shard_map/ppermute | solution.py:188
  27.7 5.7 %collective-permute-done.factor_ref = bf16[64,256]{1,0:T(8,128)(2,1)S(1)} collective-permute-done((bf16[64,256]{1,0:T(8,128)(2,1)S(1)}, bf16[64,256]{1,0:T(8,128)(2,1)S(1)}, u32[]{:S(2)}, u32[]{:S(2)}) %collective-permute-start) | collective-permute-done | bytes 32800 | tf_op jit(solution)/shard_map/ppermute | solution.py:188
  33.4 0.0 all-to-all-done.blocks_ref
  33.4 0.4 shard_map.59
  33.8 10.0 %all_to_all.20.share_ref = f32[16,32,128]{2,1,0:T(8,128)S(1)} all-to-all(f32[16,32,128]{2,1,0:T(8,128)S(1)} %get-tuple-element.14), channel_id=1, replica_groups={{0,32,64,96,128,160,192,224,256,288,320,352,384,416,448,480},{16,48,80,..., dimensions={0} | all-to-all | bytes 524288 | tf_op jit(solution)/shard_map/all_to_all | solution.py:195
  43.8 0.4 shard_map.60
  44.2 4.2 %collective-permute-start.1 = (f32[128,128]{1,0:T(8,128)S(1)}, f32[128,128]{1,0:T(8,128)S(1)}, u32[]{:S(2)}, u32[]{:S(2)}) collective-permute-start(f32[128,128]{1,0:T(8,128)S(1)} %get-tuple-element.17), channel_id=1, source_target_pairs={{0,16},{16,0},{32,48},{48,32},{64,80},{80,64},{96,112},{112,96},{1... | collective-permute-start | bytes 196616 | tf_op jit(solution)/shard_map/ppermute | solution.py:197
  48.4 0.9 collective-permute-done.1.got_ref
  49.3 0.1 shard_map.61
  49.4 8.6 %all_to_all.21.near_ref = f32[4,96,128]{2,1,0:T(8,128)S(1)} all-to-all(f32[4,96,128]{2,1,0:T(8,128)S(1)} %get-tuple-element.18), channel_id=1, replica_groups={{0,1,2,3},{4,5,6,7},{8,9,10,11},{12,13,14,15},{16,17,18,19},{20,21,22,2..., dimensions={0} | all-to-all | bytes 393216 | tf_op jit(solution)/shard_map/all_to_all | solution.py:199
  58.0 21.4 %all-gather = f32[384,128]{1,0:T(8,128)S(1)} all-gather(f32[96,128]{1,0:T(8,128)S(1)} %shard_map.62), channel_id=2, replica_groups={{0,4,8,12},{1,5,9,13},{2,6,10,14},{3,7,11,15},{16,20,24,28},{17,21,25,2..., dimensions={0}, use_global_device_ids=true | all-gather | bytes 245760 | tf_op jit(solution)/shard_map/all_gather | solution.py:201
  79.3 2.7 %shard_map.63 = (bf16[32,64,128]{2,1,0:T(8,128)(2,1)S(1)}, bf16[128,64]{1,0:T(8,128)(2,1)S(1)}) custom-call(f32[4,96,128]{2,1,0:T(8,128)S(1)} %bitcast.5, f32[128,64]{1,0:T(8,128)S(1)} %get-tuple-element.19.p_ref), custom_call_target="tpu_custom_call" | custom-call | tf_op jit(solution)/shard_map/pallas_call | solution.py:202
  82.0 20.5 %all_to_all.22.q_ref = bf16[32,64,128]{2,1,0:T(8,128)(2,1)S(1)} all-to-all(bf16[32,64,128]{2,1,0:T(8,128)(2,1)S(1)} %get-tuple-element.20), channel_id=1, replica_groups=mesh['dp'=32,'tensor'=16] {'dp'}, dimensions={0} | all-to-all | bytes 1048576 | tf_op jit(solution)/shard_map/all_to_all | solution.py:206
  102.5 1.6 %shard_map.64 = (bf16[128,4096]{1,0:T(8,128)(2,1)}, bf16[1,128,4096]{2,1,0:T(8,128)(2,1)}, f32[64,256]{1,0:T(8,128)}) custom-call(bf16[32,64,128]{2,1,0:T(8,128)(2,1)S(1)} %all_to_all.22.q_ref, bf16[128,64]{1,0:T(8,128)(2,1)S(1)} %get-tuple-element.21.p_ref, bf16[128,4096]{1,0:T(8,128)(2,1)S(1)} %fusion.rows_ref), custom_call_target="tpu_custom_call" | custom-call | tf_op jit(solution)/shard_map/pallas_call | solution.py:207
  (1 shorter events, 0.0 us)
Async XLA Ops:
  3.5 10.6 %copy-start = (bf16[256,64]{0,1:T(8,128)(2,1)S(1)}, bf16[256,64]{0,1:T(8,128)(2,1)}, u32[]{:S(2)}) copy-start(bf16[256,64]{0,1:T(8,128)(2,1)} %param.5) | copy-start | bytes 98308
  3.5 29.9 %all-to-all-start = ((bf16[32,64,256]{2,1,0:T(8,128)(2,1)}), bf16[32,64,256]{2,1,0:T(8,128)(2,1)S(1)}, u32[]{:S(2)}, u32[]{:S(2)}) async-start(bf16[32,64,256]{2,1,0:T(8,128)(2,1)} %shard_map.58), calls=%async_computation | async-start | bytes 2097152 | tf_op jit(solution)/shard_map/all_to_all | solution.py:191
  14.1 19.3 %collective-permute-start = (bf16[64,256]{1,0:T(8,128)(2,1)S(1)}, bf16[64,256]{1,0:T(8,128)(2,1)S(1)}, u32[]{:S(2)}, u32[]{:S(2)}) collective-permute-start(bf16[64,256]{1,0:T(8,128)(2,1)S(1)} %bitcast.7), channel_id=1, source_target_pairs={{0,8},{16,24},{32,7},{48,23},{96,9},{112,25},{128,6},{144,22},{384... | collective-permute-start | bytes 98312 | tf_op jit(solution)/shard_map/ppermute | solution.py:188
  44.2 5.1 %collective-permute-start.1 = (f32[128,128]{1,0:T(8,128)S(1)}, f32[128,128]{1,0:T(8,128)S(1)}, u32[]{:S(2)}, u32[]{:S(2)}) collective-permute-start(f32[128,128]{1,0:T(8,128)S(1)} %get-tuple-element.17), channel_id=1, source_target_pairs={{0,16},{16,0},{32,48},{48,32},{64,80},{80,64},{96,112},{112,96},{1... | collective-permute-start | bytes 196616 | tf_op jit(solution)/shard_map/ppermute | solution.py:197

commit v6 on v5

--- a/solution.py
+++ b/solution.py
@@ -23,6 +23,11 @@
 NEAR = [[4 * a + b for b in range(4)] for a in range(4)]
 FAR = [[4 * a + b for a in range(4)] for b in range(4)]
 SWAP = [(i, i ^ 1) for i in range(DP)]
+PAIRED = [
+    [(CORES * k + core) * DEPTH + 2 * a + b for b in range(2) for k in range(CHIPS)]
+    for a in range(DEPTH // 2)
+    for core in range(CORES)
+]
 
 
 def ring(a, b, n):
@@ -91,8 +96,13 @@
 
 
 def near_kernel(keep_ref, got_ref, share_ref, p_ref):
-    both = keep_ref[: R + 32] + got_ref[: R + 32]
-    share_ref[...] = jnp.broadcast_to(both[None], share_ref.shape)
+    both = keep_ref[:R] + got_ref[:R]
+    gram = keep_ref[R : R + 32] + got_ref[R : R + 32]
+    for half in range(2):
+        part = pack(both[:, R * half : R * (half + 1)])
+        for m in (half, half + 2):
+            share_ref[m, :32] = part
+            share_ref[m, 32:] = gram
     first = lax.rem(lax.axis_index("dp"), CORES) == 0
     mine, other = unpack(keep_ref[R + 32 :]), unpack(got_ref[R + 32 :])
     p_ref[:HALF] = jnp.where(first, mine, other)
@@ -124,7 +134,6 @@
         for j in range(8):
             pivot, row = splat_row(cols[j][0], j), splat_row(strips[s], j)
             root = lax.rsqrt(pivot)
-            root = root * (1.5 - 0.5 * pivot * root * root)
             done = jnp.where(sub == j, row * root, done)
             factors = [c * (root * root) for c in cols[j]]
             factors[0] = jnp.where(sub > j, factors[0], 0.0)
@@ -139,19 +148,30 @@
 
 def factor_kernel(far_ref, p_ref, q_ref, p_round_ref):
     both = far_ref[0] + far_ref[1] + (far_ref[2] + far_ref[3])
-    inverse = inverse_factor(unpack(both[R:]))
-    q = (dot(inverse, both[:R], ((1,), (0,)), precision=HIGH) * (1.0 / DP)).astype(BF16)
-    q_ref[...] = jnp.broadcast_to(q[None], q_ref.shape)
+    inverse = inverse_factor(unpack(both[32:]))
+    q_half = dot(inverse, unpack(both[:32]), ((1,), (0,)), precision=HIGH) * (1.0 / DP)
+    q_ref[...] = jnp.broadcast_to(pack(q_half).astype(BF16)[None], q_ref.shape)
     p_round_ref[...] = dot(p_ref[...], inverse, ((1,), (1,)), precision=HIGH).astype(BF16)
 
 
 def update_kernel(
-    q_ref, p_ref, rows_ref, update_ref, error_ref, q_new_ref, update_out, error_out, q_new_out, sems, q_sem
+    mine_ref, other_ref, p_ref, rows_ref, update_ref, error_ref, q_new_ref, update_out, error_out, q_new_out, sems, q_sem
 ):
     width = D // PARTS
     z = lax.axis_index("tensor")
+    first = lax.rem(lax.axis_index("dp"), CORES) == 0
+
+    def block(k, c):
+        even, odd = (
+            jnp.where(first if c == 0 else ~first, mine_ref[n + k].astype(F32), other_ref[n + k].astype(F32))
+            for n in (0, CHIPS)
+        )
+        upper = jnp.concatenate([even[:, :R], odd[:, :R]], 1)
+        lower = jnp.concatenate([even[:, R:], odd[:, R:]], 1)
+        return jnp.concatenate([upper, lower], 0)
+
     for c in range(CORES):
-        q_new_out[:, 128 * c : 128 * (c + 1)] = q_ref[CORES * z + c].astype(F32)
+        q_new_out[:, 128 * c : 128 * (c + 1)] = block(z, c)
     q_copy = pltpu.make_async_copy(q_new_out, q_new_ref, q_sem)
     q_copy.start()
 
@@ -164,7 +184,7 @@
 
     for n in range(PARTS):
         for k in range(n * width // COLS, (n + 1) * width // COLS):
-            q = jnp.concatenate([q_ref[CORES * k + c] for c in range(CORES)], 1)
+            q = jnp.concatenate([block(k, c) for c in range(CORES)], 1).astype(BF16)
             full = dot(p_ref[...], q, ((1,), (0,)))
             span = slice(COLS * k, COLS * (k + 1))
             update_out[:, span] = full.astype(BF16)
@@ -195,18 +215,19 @@
     part = lax.all_to_all(part, "dp", 0, 0, axis_index_groups=PLANE)
     give, keep = kernel_call(basis_kernel, out_shape=(shape(128, 128), shape(128, 128)))(part, total)
     got = lax.ppermute(give, "dp", SWAP)
-    near, p_sum = kernel_call(near_kernel, out_shape=(shape(4, R + 32, 128), shape(ROWS, R)))(keep, got)
+    near, p_sum = kernel_call(near_kernel, out_shape=(shape(4, 64, 128), shape(ROWS, R)))(keep, got)
     near = lax.all_to_all(near, "tensor", 0, 0, axis_index_groups=NEAR)
-    far = kernel_call(far_kernel, out_shape=shape(R + 32, 128))(near)
+    far = kernel_call(far_kernel, out_shape=shape(64, 128))(near)
     far = lax.all_gather(far, "tensor", axis_index_groups=FAR)
     q_blocks, p_round = kernel_call(
         factor_kernel,
-        out_shape=(shape(DP, R, 128, dtype=BF16), shape(ROWS, R, dtype=BF16)),
+        out_shape=(shape(2 * CHIPS, 32, 128, dtype=BF16), shape(ROWS, R, dtype=BF16)),
     )(far, p_sum)
-    q_blocks = lax.all_to_all(q_blocks, "dp", 0, 0)
-    update, new_error, q_mine = kernel_call(
+    q_mine = lax.all_to_all(q_blocks, ("dp", "tensor"), 0, 0, axis_index_groups=PAIRED)
+    q_other = lax.ppermute(q_mine, "dp", SWAP)
+    update, new_error, q_new = kernel_call(
         update_kernel,
-        in_specs=[vmem, vmem, vmem],
+        in_specs=[vmem, vmem, vmem, vmem],
         out_specs=[hbm, hbm, hbm],
         out_shape=(shape(ROWS, D, dtype=BF16), shape(1, ROWS, D, dtype=BF16), shape(R, COLS)),
         scratch_shapes=[
@@ -216,8 +237,8 @@
             pltpu.SemaphoreType.DMA((2, PARTS)),
             pltpu.SemaphoreType.DMA,
         ],
-    )(q_blocks, p_round, corrected)
-    return (update, new_error, q_mine.T)
+    )(q_mine, q_other, p_round, corrected)
+    return (update, new_error, q_new.T)
 
 
 def solution(mesh):

time: 105 us -> 102 us (0.971)
  blocking collectives: 60.4 us -> 49.5 us
  starting transfers between devices: 28.4 us -> 36 us
  waiting for transfers between devices: 6.63 us -> 7.77 us
    all_to_all x1, blocking collectives: 20.5 us -> 12.3 us  [body(): lax.all_to_all(q_blocks, ('dp', 'tensor'), 0, 0, axis_index_groups=PAIRED)]
    ppermute x0 -> x1, starting transfers between devices: none -> 7.69 us  [body(): q_other = lax.ppermute(q_mine, 'dp', SWAP)]
    all_to_all x1, blocking collectives: 8.58 us -> 7.19 us  [body(): near = lax.all_to_all(near, 'tensor', 0, 0, axis_index_groups=NEAR)]
    all_gather x1, blocking collectives: 21.4 us -> 20.1 us  [body(): far = lax.all_gather(far, 'tensor', axis_index_groups=FAR)]
    ppermute x0 -> x1, waiting for transfers between devices: none -> 1.14 us  [body(): q_other = lax.ppermute(q_mine, 'dp', SWAP)]
  transfers between devices with their start and end apart: 3 -> 4, of which waited for: 2 -> 3; matrix products, arithmetic and copies ran while one was open for 0% -> 0% of each run, Pallas kernels for 0% -> 0%
where the time goes in v6:
time: 102 us
  blocking collectives  49.5 us (49%)
  starting transfers between devices  36 us (35%)
  waiting for transfers between devices  7.77 us (8%)
  Pallas kernels  5.94 us (6%)
  other arithmetic  1.79 us (2%)
    all_gather x1, blocking collectives, body(): far = lax.all_gather(far, 'tensor', axis_index_groups=FAR)  20.1 us
    ppermute x1, starting transfers between devices, body(): factor_t = lax.ppermute(q_start.T, ('dp', 'tensor'), factor_route())  13.6 us
    all_to_all x1, blocking collectives, body(): lax.all_to_all(q_blocks, ('dp', 'tensor'), 0, 0, axis_index_groups=PAIRED)  12.3 us
    all_to_all x1, starting transfers between devices, body(): blocks = lax.all_to_all(blocks, 'dp', 0, 0)  10.6 us
    all_to_all x1, blocking collectives, body(): part = lax.all_to_all(part, 'dp', 0, 0, axis_index_groups=PLANE)  9.96 us
    ppermute x1, starting transfers between devices, body(): q_other = lax.ppermute(q_mine, 'dp', SWAP)  7.69 us
    all_to_all x1, blocking collectives, body(): near = lax.all_to_all(near, 'tensor', 0, 0, axis_index_groups=NEAR)  7.19 us
    ppermute x1, waiting for transfers between devices, body(): factor_t = lax.ppermute(q_start.T, ('dp', 'tensor'), factor_route())  5.74 us
  transfers between devices with their start and end apart: 4, of which 3 were waited for; matrix products, arithmetic and copies ran while one was open for 0% of the time, Pallas kernels for 0%

profile of v6, /device:TPU:1, one launch (start us, length us, event | category | flops | bytes accessed | tf_op | source)
XLA Modules:
  0.0 101.8 jit_solution(8463210832234881910)
XLA Ops:
  0.6 1.8 %fusion.rows_ref = bf16[128,4096]{1,0:T(8,128)(2,1)S(1)} fusion(bf16[1,128,4096]{2,1,0:T(8,128)(2,1)} %param.4, bf16[1,128,4096]{2,1,0:T(8,128)(2,1)} %param.3), kind=kLoop, calls=%fused_computation.1 | loop fusion | flops 2097152 | bytes 3145728 | tf_op jit(solution)/shard_map/convert_element_type | solution.py:209
  2.4 1.0 %shard_map.58 = bf16[32,64,256]{2,1,0:T(8,128)(2,1)} custom-call(bf16[128,4096]{1,0:T(8,128)(2,1)S(1)} %fusion.rows_ref), custom_call_target="tpu_custom_call" | custom-call | tf_op jit(solution)/shard_map/pallas_call | solution.py:210
  3.5 0.0 copy-start
  3.5 10.6 %all-to-all-start = ((bf16[32,64,256]{2,1,0:T(8,128)(2,1)}), bf16[32,64,256]{2,1,0:T(8,128)(2,1)S(1)}, u32[]{:S(2)}, u32[]{:S(2)}) async-start(bf16[32,64,256]{2,1,0:T(8,128)(2,1)} %shard_map.58), calls=%async_computation | async-start | bytes 2097152 | tf_op jit(solution)/shard_map/all_to_all | solution.py:211
  14.1 0.0 copy-done
  14.1 13.6 %collective-permute-start = (bf16[64,256]{1,0:T(8,128)(2,1)S(1)}, bf16[64,256]{1,0:T(8,128)(2,1)S(1)}, u32[]{:S(2)}, u32[]{:S(2)}) collective-permute-start(bf16[64,256]{1,0:T(8,128)(2,1)S(1)} %bitcast.7), channel_id=1, source_target_pairs={{0,8},{16,24},{32,7},{48,23},{96,9},{112,25},{128,6},{144,22},{384... | collective-permute-start | bytes 98312 | tf_op jit(solution)/shard_map/ppermute | solution.py:208
  27.7 5.7 %collective-permute-done.factor_ref = bf16[64,256]{1,0:T(8,128)(2,1)S(1)} collective-permute-done((bf16[64,256]{1,0:T(8,128)(2,1)S(1)}, bf16[64,256]{1,0:T(8,128)(2,1)S(1)}, u32[]{:S(2)}, u32[]{:S(2)}) %collective-permute-start) | collective-permute-done | bytes 32800 | tf_op jit(solution)/shard_map/ppermute | solution.py:208
  33.4 0.0 all-to-all-done.blocks_ref
  33.4 0.4 shard_map.59
  33.8 10.0 %all_to_all.20.share_ref = f32[16,32,128]{2,1,0:T(8,128)S(1)} all-to-all(f32[16,32,128]{2,1,0:T(8,128)S(1)} %get-tuple-element.14), channel_id=1, replica_groups={{0,32,64,96,128,160,192,224,256,288,320,352,384,416,448,480},{16,48,80,..., dimensions={0} | all-to-all | bytes 524288 | tf_op jit(solution)/shard_map/all_to_all | solution.py:215
  43.8 0.4 shard_map.60
  44.2 4.2 %collective-permute-start.1 = (f32[128,128]{1,0:T(8,128)S(1)}, f32[128,128]{1,0:T(8,128)S(1)}, u32[]{:S(2)}, u32[]{:S(2)}) collective-permute-start(f32[128,128]{1,0:T(8,128)S(1)} %get-tuple-element.17), channel_id=1, source_target_pairs={{0,16},{16,0},{32,48},{48,32},{64,80},{80,64},{96,112},{112,96},{1... | collective-permute-start | bytes 196616 | tf_op jit(solution)/shard_map/ppermute | solution.py:217
  48.4 0.9 collective-permute-done.1.got_ref
  49.3 0.1 shard_map.61
  49.4 7.2 %all_to_all.21.near_ref = f32[4,64,128]{2,1,0:T(8,128)S(1)} all-to-all(f32[4,64,128]{2,1,0:T(8,128)S(1)} %get-tuple-element.18), channel_id=1, replica_groups={{0,1,2,3},{4,5,6,7},{8,9,10,11},{12,13,14,15},{16,17,18,19},{20,21,22,2..., dimensions={0} | all-to-all | bytes 262144 | tf_op jit(solution)/shard_map/all_to_all | solution.py:219
  56.6 20.1 %all-gather = f32[256,128]{1,0:T(8,128)S(1)} all-gather(f32[64,128]{1,0:T(8,128)S(1)} %shard_map.62), channel_id=2, replica_groups={{0,4,8,12},{1,5,9,13},{2,6,10,14},{3,7,11,15},{16,20,24,28},{17,21,25,2..., dimensions={0}, use_global_device_ids=true | all-gather | bytes 163840 | tf_op jit(solution)/shard_map/all_gather | solution.py:221
  76.7 2.2 %shard_map.63 = (bf16[32,32,128]{2,1,0:T(8,128)(2,1)S(1)}, bf16[128,64]{1,0:T(8,128)(2,1)S(1)}) custom-call(f32[4,64,128]{2,1,0:T(8,128)S(1)} %bitcast.5, f32[128,64]{1,0:T(8,128)S(1)} %get-tuple-element.19.p_ref), custom_call_target="tpu_custom_call" | custom-call | tf_op jit(solution)/shard_map/pallas_call | solution.py:222
  78.9 12.3 %all_to_all.22.mine_ref = bf16[32,32,128]{2,1,0:T(8,128)(2,1)S(1)} all-to-all(bf16[32,32,128]{2,1,0:T(8,128)(2,1)S(1)} %get-tuple-element.20), channel_id=1, replica_groups={{0,32,64,96,128,160,192,224,256,288,320,352,384,416,448,480,1,33,65,97,..., dimensions={0} | all-to-all | bytes 524288 | tf_op jit(solution)/shard_map/all_to_all | solution.py:226
  91.2 7.7 %collective-permute-start.2 = (bf16[32,32,128]{2,1,0:T(8,128)(2,1)S(1)}, bf16[32,32,128]{2,1,0:T(8,128)(2,1)S(1)}, u32[]{:S(2)}, u32[]{:S(2)}) collective-permute-start(bf16[32,32,128]{2,1,0:T(8,128)(2,1)S(1)} %all_to_all.22.mine_ref), channel_id=1, source_target_pairs={{0,16},{16,0},{32,48},{48,32},{64,80},{80,64},{96,112},{112,96},{1... | collective-permute-start | bytes 786440 | tf_op jit(solution)/shard_map/ppermute | solution.py:227
  98.9 1.1 %collective-permute-done.2.other_ref = bf16[32,32,128]{2,1,0:T(8,128)(2,1)S(1)} collective-permute-done((bf16[32,32,128]{2,1,0:T(8,128)(2,1)S(1)}, bf16[32,32,128]{2,1,0:T(8,128)(2,1)S(1)}, u32[]{:S(2)}, u32[]{:S(2)}) %collective-permute-start.2) | collective-permute-done | bytes 262176 | tf_op jit(solution)/shard_map/ppermute | solution.py:227
  100.0 1.7 %shard_map.64 = (bf16[128,4096]{1,0:T(8,128)(2,1)}, bf16[1,128,4096]{2,1,0:T(8,128)(2,1)}, f32[64,256]{1,0:T(8,128)}) custom-call(bf16[32,32,128]{2,1,0:T(8,128)(2,1)S(1)} %all_to_all.22.mine_ref, bf16[32,32,128]{2,1,0:T(8,128)(2,1)S(1)} %collective-permute-done.2.other_ref, bf16[128,64]{1,0:T(8,128)(2,1)S(1)} %get-tuple-element.21.p_ref, ...), custom_call_target="tpu_custom_call" | custom-call | tf_op jit(solution)/shard_map/pallas_call | solution.py:228
  (1 shorter events, 0.0 us)
Async XLA Ops:
  3.5 10.6 %copy-start = (bf16[256,64]{0,1:T(8,128)(2,1)S(1)}, bf16[256,64]{0,1:T(8,128)(2,1)}, u32[]{:S(2)}) copy-start(bf16[256,64]{0,1:T(8,128)(2,1)} %param.5) | copy-start | bytes 98308
  3.5 29.9 %all-to-all-start = ((bf16[32,64,256]{2,1,0:T(8,128)(2,1)}), bf16[32,64,256]{2,1,0:T(8,128)(2,1)S(1)}, u32[]{:S(2)}, u32[]{:S(2)}) async-start(bf16[32,64,256]{2,1,0:T(8,128)(2,1)} %shard_map.58), calls=%async_computation | async-start | bytes 2097152 | tf_op jit(solution)/shard_map/all_to_all | solution.py:211
  14.1 19.3 %collective-permute-start = (bf16[64,256]{1,0:T(8,128)(2,1)S(1)}, bf16[64,256]{1,0:T(8,128)(2,1)S(1)}, u32[]{:S(2)}, u32[]{:S(2)}) collective-permute-start(bf16[64,256]{1,0:T(8,128)(2,1)S(1)} %bitcast.7), channel_id=1, source_target_pairs={{0,8},{16,24},{32,7},{48,23},{96,9},{112,25},{128,6},{144,22},{384... | collective-permute-start | bytes 98312 | tf_op jit(solution)/shard_map/ppermute | solution.py:208
  44.2 5.1 %collective-permute-start.1 = (f32[128,128]{1,0:T(8,128)S(1)}, f32[128,128]{1,0:T(8,128)S(1)}, u32[]{:S(2)}, u32[]{:S(2)}) collective-permute-start(f32[128,128]{1,0:T(8,128)S(1)} %get-tuple-element.17), channel_id=1, source_target_pairs={{0,16},{16,0},{32,48},{48,32},{64,80},{80,64},{96,112},{112,96},{1... | collective-permute-start | bytes 196616 | tf_op jit(solution)/shard_map/ppermute | solution.py:217
  91.2 8.8 %collective-permute-start.2 = (bf16[32,32,128]{2,1,0:T(8,128)(2,1)S(1)}, bf16[32,32,128]{2,1,0:T(8,128)(2,1)S(1)}, u32[]{:S(2)}, u32[]{:S(2)}) collective-permute-start(bf16[32,32,128]{2,1,0:T(8,128)(2,1)S(1)} %all_to_all.22.mine_ref), channel_id=1, source_target_pairs={{0,16},{16,0},{32,48},{48,32},{64,80},{80,64},{96,112},{112,96},{1... | collective-permute-start | bytes 786440 | tf_op jit(solution)/shard_map/ppermute | solution.py:227

commit v7 on v6

--- a/solution.py
+++ b/solution.py
@@ -15,6 +15,7 @@
 D = 4096
 COLS = D // CHIPS
 R = 64
+GRAM = 24
 PARTS = 4
 HIGH = lax.Precision.HIGHEST
 F32, BF16 = jnp.float32, jnp.bfloat16
@@ -56,6 +57,23 @@
     return jnp.concatenate([x[:32, :R], x[32:, :R]], 1)
 
 
+def fold(gram):
+    corners = (gram[:32, :32], gram[:32, 32:], gram[32:, 32:])
+    return jnp.concatenate(
+        [jnp.concatenate([x[8 * n : 8 * n + 8] for n in range(4)], 1) for x in corners], 0
+    )
+
+
+def unfold(x):
+    a, b, c = (
+        jnp.concatenate([x[8 * m : 8 * m + 8, 32 * n : 32 * n + 32] for n in range(4)], 0)
+        for m in range(3)
+    )
+    upper = jnp.concatenate([jnp.concatenate([a, b], 1), jnp.concatenate([jnp.zeros_like(b), c], 1)], 0)
+    rows = lax.broadcasted_iota(jnp.int32, (R, R), 0)
+    return jnp.where((rows >= 32) & (lax.broadcasted_iota(jnp.int32, (R, R), 1) < 32), upper.T, upper)
+
+
 def unpack(x):
     return jnp.concatenate([x[:, :R], x[:, R:]], 0)
 
@@ -64,10 +82,35 @@
     return lax.dot_general(a, b, (over, ((), ())), preferred_element_type=F32, **kw)
 
 
-def block_kernel(rows_ref, out_ref):
-    for k in range(CHIPS):
-        for c in range(CORES):
-            out_ref[CORES * k + c] = rows_ref[HALF * c : HALF * (c + 1), COLS * k : COLS * (k + 1)]
+def block_kernel(grad_ref, error_ref, out_ref, grad_in, error_in, blocks, in_sems, out_sems):
+    size = ROWS // PARTS
+
+    def arrivals(n):
+        rows = pl.ds(n * size, size)
+        return [
+            pltpu.make_async_copy(grad_ref.at[0, rows], grad_in.at[rows], in_sems.at[0, n]),
+            pltpu.make_async_copy(error_ref.at[0, rows], error_in.at[rows], in_sems.at[1, n]),
+        ]
+
+    def departure(c):
+        return pltpu.make_async_copy(blocks.at[:, c], out_ref.at[:, c], out_sems.at[c])
+
+    for n in range(PARTS):
+        for copy in arrivals(n):
+            copy.start()
+    for n in range(PARTS):
+        for copy in arrivals(n):
+            copy.wait()
+        c, row = divmod(n * size, HALF)
+        rows = slice(n * size, (n + 1) * size)
+        for k in range(CHIPS):
+            span = slice(COLS * k, COLS * (k + 1))
+            x = grad_in[rows, span].astype(F32) + error_in[rows, span].astype(F32)
+            blocks[k, c, row : row + size] = x.astype(BF16)
+        if row + size == HALF:
+            departure(c).start()
+    for c in range(CORES):
+        departure(c).wait()
 
 
 def sketch_kernel(blocks_ref, factor_ref, total_ref, share_ref):
@@ -87,24 +130,24 @@
     first = lax.rem(lax.axis_index("dp"), CORES) == 0
     left = dot(p, total_ref[:, :128], ((0,), (0,)), precision=HIGH)
     right = dot(p, total_ref[:, 128:], ((0,), (0,)), precision=HIGH)
-    gram = pack(dot(p, p, ((0,), (0,)), precision=HIGH))
+    gram = fold(dot(p, p, ((0,), (0,)), precision=HIGH))
     keep_ref[:R] = jnp.where(first, left, right)
     give_ref[:R] = jnp.where(first, right, left)
     for ref in (keep_ref, give_ref):
-        ref[R : R + 32] = gram
-        ref[R + 32 :] = packed
+        ref[R : R + GRAM] = gram
+        ref[R + GRAM :] = packed
 
 
 def near_kernel(keep_ref, got_ref, share_ref, p_ref):
     both = keep_ref[:R] + got_ref[:R]
-    gram = keep_ref[R : R + 32] + got_ref[R : R + 32]
+    gram = keep_ref[R : R + GRAM] + got_ref[R : R + GRAM]
     for half in range(2):
         part = pack(both[:, R * half : R * (half + 1)])
         for m in (half, half + 2):
             share_ref[m, :32] = part
             share_ref[m, 32:] = gram
     first = lax.rem(lax.axis_index("dp"), CORES) == 0
-    mine, other = unpack(keep_ref[R + 32 :]), unpack(got_ref[R + 32 :])
+    mine, other = unpack(keep_ref[R + GRAM :]), unpack(got_ref[R + GRAM :])
     p_ref[:HALF] = jnp.where(first, mine, other)
     p_ref[HALF:] = jnp.where(first, other, mine)
 
@@ -148,7 +191,7 @@
 
 def factor_kernel(far_ref, p_ref, q_ref, p_round_ref):
     both = far_ref[0] + far_ref[1] + (far_ref[2] + far_ref[3])
-    inverse = inverse_factor(unpack(both[32:]))
+    inverse = inverse_factor(unfold(both[32:]))
     q_half = dot(inverse, unpack(both[:32]), ((1,), (0,)), precision=HIGH) * (1.0 / DP)
     q_ref[...] = jnp.broadcast_to(pack(q_half).astype(BF16)[None], q_ref.shape)
     p_round_ref[...] = dot(p_ref[...], inverse, ((1,), (1,)), precision=HIGH).astype(BF16)
@@ -163,7 +206,7 @@
 
     def block(k, c):
         even, odd = (
-            jnp.where(first if c == 0 else ~first, mine_ref[n + k].astype(F32), other_ref[n + k].astype(F32))
+            jnp.where(first if c == 0 else ~first, mine_ref[n + k], other_ref[n + k])
             for n in (0, CHIPS)
         )
         upper = jnp.concatenate([even[:, :R], odd[:, :R]], 1)
@@ -171,7 +214,7 @@
         return jnp.concatenate([upper, lower], 0)
 
     for c in range(CORES):
-        q_new_out[:, 128 * c : 128 * (c + 1)] = block(z, c)
+        q_new_out[:, 128 * c : 128 * (c + 1)] = block(z, c).astype(F32)
     q_copy = pltpu.make_async_copy(q_new_out, q_new_ref, q_sem)
     q_copy.start()
 
@@ -184,7 +227,7 @@
 
     for n in range(PARTS):
         for k in range(n * width // COLS, (n + 1) * width // COLS):
-            q = jnp.concatenate([block(k, c) for c in range(CORES)], 1).astype(BF16)
+            q = jnp.concatenate([block(k, c) for c in range(CORES)], 1)
             full = dot(p_ref[...], q, ((1,), (0,)))
             span = slice(COLS * k, COLS * (k + 1))
             update_out[:, span] = full.astype(BF16)
@@ -207,17 +250,30 @@
     vmem, hbm = pl.BlockSpec(memory_space=pltpu.VMEM), pl.BlockSpec(memory_space=pltpu.HBM)
     factor_t = lax.ppermute(q_start.T, ("dp", "tensor"), factor_route())
     corrected = (grad[0].astype(F32) + error[0].astype(F32)).astype(BF16)
-    blocks = kernel_call(block_kernel, out_shape=shape(DP, HALF, COLS, dtype=BF16))(corrected)
-    blocks = lax.all_to_all(blocks, "dp", 0, 0)
+    blocks = kernel_call(
+        block_kernel,
+        mib=56,
+        in_specs=[hbm, hbm],
+        out_specs=hbm,
+        out_shape=shape(CHIPS, CORES, HALF, COLS, dtype=BF16),
+        scratch_shapes=[
+            pltpu.VMEM((ROWS, D), BF16),
+            pltpu.VMEM((ROWS, D), BF16),
+            pltpu.VMEM((CHIPS, CORES, HALF, COLS), BF16),
+            pltpu.SemaphoreType.DMA((2, PARTS)),
+            pltpu.SemaphoreType.DMA((CORES,)),
+        ],
+    )(grad, error)
+    blocks = lax.all_to_all(blocks.reshape(DP, HALF, COLS), "dp", 0, 0)
     total, part = kernel_call(
         sketch_kernel, out_shape=(shape(HALF, COLS), shape(CHIPS, 32, 128))
     )(blocks, factor_t)
     part = lax.all_to_all(part, "dp", 0, 0, axis_index_groups=PLANE)
-    give, keep = kernel_call(basis_kernel, out_shape=(shape(128, 128), shape(128, 128)))(part, total)
+    give, keep = kernel_call(basis_kernel, out_shape=(shape(R + GRAM + 32, 128),) * 2)(part, total)
     got = lax.ppermute(give, "dp", SWAP)
-    near, p_sum = kernel_call(near_kernel, out_shape=(shape(4, 64, 128), shape(ROWS, R)))(keep, got)
+    near, p_sum = kernel_call(near_kernel, out_shape=(shape(4, 32 + GRAM, 128), shape(ROWS, R)))(keep, got)
     near = lax.all_to_all(near, "tensor", 0, 0, axis_index_groups=NEAR)
-    far = kernel_call(far_kernel, out_shape=shape(64, 128))(near)
+    far = kernel_call(far_kernel, out_shape=shape(32 + GRAM, 128))(near)
     far = lax.all_gather(far, "tensor", axis_index_groups=FAR)
     q_blocks, p_round = kernel_call(
         factor_kernel,

time: 102 us -> 102 us (level)
  other arithmetic: 1.79 us -> 0.25 us
  Pallas kernels: 5.94 us -> 7.46 us
    convert_element_type x1, other arithmetic: 1.79 us -> 0.25 us  [body(): corrected = (grad[0].astype(F32) + error[0].astype(F32)).astype(BF16)]
    pallas_call x4, Pallas kernels: 1.56 us -> 2.96 us  [the longest x1 2.45 us: body(): kernel_call(block_kernel, mib=56, in_specs=[hbm, hbm], out_specs=hbm, out...]
where the time goes in v7:
time: 102 us; the launch traced here: 101 us
  blocking collectives  49.3 us (48%)
  starting transfers between devices  36.1 us (35%)
  waiting for transfers between devices  7.49 us (7%)
  Pallas kernels  7.46 us (7%)
    all_gather x1, blocking collectives, body(): far = lax.all_gather(far, 'tensor', axis_index_groups=FAR)  19.9 us
    ppermute x1, starting transfers between devices, body(): factor_t = lax.ppermute(q_start.T, ('dp', 'tensor'), factor_route())  13.6 us
    all_to_all x1, blocking collectives, body(): lax.all_to_all(q_blocks, ('dp', 'tensor'), 0, 0, axis_index_groups=PAIRED)  12.1 us
    all_to_all x1, starting transfers between devices, body(): blocks = lax.all_to_all(blocks.reshape(DP, HALF, COLS), 'dp', 0, 0)  10.5 us
    all_to_all x1, blocking collectives, body(): part = lax.all_to_all(part, 'dp', 0, 0, axis_index_groups=PLANE)  10.1 us
    ppermute x1, starting transfers between devices, body(): q_other = lax.ppermute(q_mine, 'dp', SWAP)  7.81 us
    all_to_all x1, blocking collectives, body(): near = lax.all_to_all(near, 'tensor', 0, 0, axis_index_groups=NEAR)  7.13 us
    ppermute x1, waiting for transfers between devices, body(): factor_t = lax.ppermute(q_start.T, ('dp', 'tensor'), factor_route())  5.74 us
  transfers between devices with their start and end apart: 4, of which 3 were waited for; matrix products, arithmetic and copies ran while one was open for 0% of the time, Pallas kernels for 0%

profile of v7, /device:TPU:1, one launch (start us, length us, event | category | flops | bytes accessed | tf_op | source)
XLA Modules:
  0.0 101.3 jit_solution(16270546936057172899)
XLA Ops:
  0.6 2.4 %shard_map.58 = bf16[16,2,64,256]{3,2,1,0:T(8,128)(2,1)} custom-call(bf16[1,128,4096]{2,1,0:T(8,128)(2,1)} %grad_ref.1, bf16[1,128,4096]{2,1,0:T(8,128)(2,1)} %error_ref.1), custom_call_target="tpu_custom_call" | custom-call | tf_op jit(solution)/shard_map/pallas_call | solution.py:253
  3.1 0.0 copy-start.2
  3.1 10.5 %all-to-all-start = ((bf16[32,64,256]{2,1,0:T(8,128)(2,1)}), bf16[32,64,256]{2,1,0:T(8,128)(2,1)S(1)}, u32[]{:S(2)}, u32[]{:S(2)}) async-start(bf16[32,64,256]{2,1,0:T(8,128)(2,1)} %bitcast.7), calls=%async_computation | async-start | bytes 2097152 | tf_op jit(solution)/shard_map/all_to_all | solution.py:267
  13.6 0.0 copy-done.2
  13.6 13.6 %collective-permute-start = (bf16[64,256]{1,0:T(8,128)(2,1)S(1)}, bf16[64,256]{1,0:T(8,128)(2,1)S(1)}, u32[]{:S(2)}, u32[]{:S(2)}) collective-permute-start(bf16[64,256]{1,0:T(8,128)(2,1)S(1)} %bitcast.9), channel_id=1, source_target_pairs={{0,8},{16,24},{32,7},{48,23},{96,9},{112,25},{128,6},{144,22},{384... | collective-permute-start | bytes 98312 | tf_op jit(solution)/shard_map/ppermute | solution.py:251
  27.2 5.7 %collective-permute-done.factor_ref = bf16[64,256]{1,0:T(8,128)(2,1)S(1)} collective-permute-done((bf16[64,256]{1,0:T(8,128)(2,1)S(1)}, bf16[64,256]{1,0:T(8,128)(2,1)S(1)}, u32[]{:S(2)}, u32[]{:S(2)}) %collective-permute-start) | collective-permute-done | bytes 32800 | tf_op jit(solution)/shard_map/ppermute | solution.py:251
  32.9 0.0 all-to-all-done.blocks_ref
  32.9 0.4 shard_map.59
  33.3 0.0 copy-start
  33.4 0.0 copy-start.1
  33.4 10.1 %all_to_all.20.share_ref = f32[16,32,128]{2,1,0:T(8,128)S(1)} all-to-all(f32[16,32,128]{2,1,0:T(8,128)S(1)} %get-tuple-element.14), channel_id=1, replica_groups={{0,32,64,96,128,160,192,224,256,288,320,352,384,416,448,480},{16,48,80,..., dimensions={0} | all-to-all | bytes 524288 | tf_op jit(solution)/shard_map/all_to_all | solution.py:271
  43.5 0.4 shard_map.60
  43.9 4.2 %collective-permute-start.1 = (f32[120,128]{1,0:T(8,128)S(1)}, f32[120,128]{1,0:T(8,128)S(1)}, u32[]{:S(2)}, u32[]{:S(2)}) collective-permute-start(f32[120,128]{1,0:T(8,128)S(1)} %get-tuple-element.17), channel_id=1, source_target_pairs={{0,16},{16,0},{32,48},{48,32},{64,80},{80,64},{96,112},{112,96},{1... | collective-permute-start | bytes 184328 | tf_op jit(solution)/shard_map/ppermute | solution.py:273
  48.1 0.9 collective-permute-done.1.got_ref
  49.0 0.1 shard_map.61
  49.1 7.1 %all_to_all.21.near_ref = f32[4,56,128]{2,1,0:T(8,128)S(1)} all-to-all(f32[4,56,128]{2,1,0:T(8,128)S(1)} %get-tuple-element.18), channel_id=1, replica_groups={{0,1,2,3},{4,5,6,7},{8,9,10,11},{12,13,14,15},{16,17,18,19},{20,21,22,2..., dimensions={0} | all-to-all | bytes 229376 | tf_op jit(solution)/shard_map/all_to_all | solution.py:275
  56.2 19.9 %all-gather = f32[224,128]{1,0:T(8,128)S(1)} all-gather(f32[56,128]{1,0:T(8,128)S(1)} %shard_map.62), channel_id=2, replica_groups={{0,4,8,12},{1,5,9,13},{2,6,10,14},{3,7,11,15},{16,20,24,28},{17,21,25,2..., dimensions={0}, use_global_device_ids=true | all-gather | bytes 143360 | tf_op jit(solution)/shard_map/all_gather | solution.py:277
  76.2 2.4 %shard_map.63 = (bf16[32,32,128]{2,1,0:T(8,128)(2,1)S(1)}, bf16[128,64]{1,0:T(8,128)(2,1)S(1)}) custom-call(f32[4,56,128]{2,1,0:T(8,128)S(1)} %bitcast.6, f32[128,64]{1,0:T(8,128)S(1)} %get-tuple-element.19.p_ref), custom_call_target="tpu_custom_call" | custom-call | tf_op jit(solution)/shard_map/pallas_call | solution.py:278
  78.5 12.1 %all_to_all.22.mine_ref = bf16[32,32,128]{2,1,0:T(8,128)(2,1)S(1)} all-to-all(bf16[32,32,128]{2,1,0:T(8,128)(2,1)S(1)} %get-tuple-element.20), channel_id=1, replica_groups={{0,32,64,96,128,160,192,224,256,288,320,352,384,416,448,480,1,33,65,97,..., dimensions={0} | all-to-all | bytes 524288 | tf_op jit(solution)/shard_map/all_to_all | solution.py:282
  90.7 7.8 %collective-permute-start.2 = (bf16[32,32,128]{2,1,0:T(8,128)(2,1)S(1)}, bf16[32,32,128]{2,1,0:T(8,128)(2,1)S(1)}, u32[]{:S(2)}, u32[]{:S(2)}) collective-permute-start(bf16[32,32,128]{2,1,0:T(8,128)(2,1)S(1)} %all_to_all.22.mine_ref), channel_id=1, source_target_pairs={{0,16},{16,0},{32,48},{48,32},{64,80},{80,64},{96,112},{112,96},{1... | collective-permute-start | bytes 786440 | tf_op jit(solution)/shard_map/ppermute | solution.py:283
  98.5 0.0 copy-done
  98.5 0.0 copy-done.1
  98.5 0.2 fusion.rows_ref
  98.7 0.9 collective-permute-done.2.other_ref
  99.6 1.7 %shard_map.64 = (bf16[128,4096]{1,0:T(8,128)(2,1)}, bf16[1,128,4096]{2,1,0:T(8,128)(2,1)}, f32[64,256]{1,0:T(8,128)}) custom-call(bf16[32,32,128]{2,1,0:T(8,128)(2,1)S(1)} %all_to_all.22.mine_ref, bf16[32,32,128]{2,1,0:T(8,128)(2,1)S(1)} %collective-permute-done.2.other_ref, bf16[128,64]{1,0:T(8,128)(2,1)S(1)} %get-tuple-element.21.p_ref, ...), custom_call_target="tpu_custom_call" | custom-call | tf_op jit(solution)/shard_map/pallas_call | solution.py:284
  (1 shorter events, 0.0 us)
Async XLA Ops:
  3.1 10.5 %copy-start.2 = (bf16[256,64]{0,1:T(8,128)(2,1)S(1)}, bf16[256,64]{0,1:T(8,128)(2,1)}, u32[]{:S(2)}) copy-start(bf16[256,64]{0,1:T(8,128)(2,1)} %param.5) | copy-start | bytes 98308
  3.1 29.8 %all-to-all-start = ((bf16[32,64,256]{2,1,0:T(8,128)(2,1)}), bf16[32,64,256]{2,1,0:T(8,128)(2,1)S(1)}, u32[]{:S(2)}, u32[]{:S(2)}) async-start(bf16[32,64,256]{2,1,0:T(8,128)(2,1)} %bitcast.7), calls=%async_computation | async-start | bytes 2097152 | tf_op jit(solution)/shard_map/all_to_all | solution.py:267
  13.6 19.3 %collective-permute-start = (bf16[64,256]{1,0:T(8,128)(2,1)S(1)}, bf16[64,256]{1,0:T(8,128)(2,1)S(1)}, u32[]{:S(2)}, u32[]{:S(2)}) collective-permute-start(bf16[64,256]{1,0:T(8,128)(2,1)S(1)} %bitcast.9), channel_id=1, source_target_pairs={{0,8},{16,24},{32,7},{48,23},{96,9},{112,25},{128,6},{144,22},{384... | collective-permute-start | bytes 98312 | tf_op jit(solution)/shard_map/ppermute | solution.py:251
  33.3 65.1 %copy-start = (bf16[1,128,4096]{2,1,0:T(8,128)(2,1)S(1)}, bf16[1,128,4096]{2,1,0:T(8,128)(2,1)}, u32[]{:S(2)}) copy-start(bf16[1,128,4096]{2,1,0:T(8,128)(2,1)} %grad_ref.1) | copy-start | bytes 3145732
  33.4 65.1 %copy-start.1 = (bf16[1,128,4096]{2,1,0:T(8,128)(2,1)S(1)}, bf16[1,128,4096]{2,1,0:T(8,128)(2,1)}, u32[]{:S(2)}) copy-start(bf16[1,128,4096]{2,1,0:T(8,128)(2,1)} %error_ref.1) | copy-start | bytes 3145732
  43.9 5.1 %collective-permute-start.1 = (f32[120,128]{1,0:T(8,128)S(1)}, f32[120,128]{1,0:T(8,128)S(1)}, u32[]{:S(2)}, u32[]{:S(2)}) collective-permute-start(f32[120,128]{1,0:T(8,128)S(1)} %get-tuple-element.17), channel_id=1, source_target_pairs={{0,16},{16,0},{32,48},{48,32},{64,80},{80,64},{96,112},{112,96},{1... | collective-permute-start | bytes 184328 | tf_op jit(solution)/shard_map/ppermute | solution.py:273
  90.7 9.0 %collective-permute-start.2 = (bf16[32,32,128]{2,1,0:T(8,128)(2,1)S(1)}, bf16[32,32,128]{2,1,0:T(8,128)(2,1)S(1)}, u32[]{:S(2)}, u32[]{:S(2)}) collective-permute-start(bf16[32,32,128]{2,1,0:T(8,128)(2,1)S(1)} %all_to_all.22.mine_ref), channel_id=1, source_target_pairs={{0,16},{16,0},{32,48},{48,32},{64,80},{80,64},{96,112},{112,96},{1... | collective-permute-start | bytes 786440 | tf_op jit(solution)/shard_map/ppermute | solution.py:283

commit v8 on v7

--- a/solution.py
+++ b/solution.py
@@ -190,7 +190,7 @@
 
 
 def factor_kernel(far_ref, p_ref, q_ref, p_round_ref):
-    both = far_ref[0] + far_ref[1] + (far_ref[2] + far_ref[3])
+    both = far_ref[:, :128] + far_ref[:, 128:256] + (far_ref[:, 256:384] + far_ref[:, 384:])
     inverse = inverse_factor(unfold(both[32:]))
     q_half = dot(inverse, unpack(both[:32]), ((1,), (0,)), precision=HIGH) * (1.0 / DP)
     q_ref[...] = jnp.broadcast_to(pack(q_half).astype(BF16)[None], q_ref.shape)
@@ -274,7 +274,7 @@
     near, p_sum = kernel_call(near_kernel, out_shape=(shape(4, 32 + GRAM, 128), shape(ROWS, R)))(keep, got)
     near = lax.all_to_all(near, "tensor", 0, 0, axis_index_groups=NEAR)
     far = kernel_call(far_kernel, out_shape=shape(32 + GRAM, 128))(near)
-    far = lax.all_gather(far, "tensor", axis_index_groups=FAR)
+    far = lax.all_gather(far, "tensor", axis_index_groups=FAR, axis=1, tiled=True)
     q_blocks, p_round = kernel_call(
         factor_kernel,
         out_shape=(shape(2 * CHIPS, 32, 128, dtype=BF16), shape(ROWS, R, dtype=BF16)),

time: 102 us -> 102 us (level)
  no operation moved by 1% of the time
where the time goes in v8:
time: 102 us; the launch traced here: 101 us
  blocking collectives  49.3 us (48%)
  starting transfers between devices  36.1 us (35%)
  waiting for transfers between devices  7.49 us (7%)
  Pallas kernels  7.46 us (7%)
    all_gather x1, blocking collectives, body(): lax.all_gather(far, 'tensor', axis_index_groups=FAR, axis=1, tiled=True)  19.9 us
    ppermute x1, starting transfers between devices, body(): factor_t = lax.ppermute(q_start.T, ('dp', 'tensor'), factor_route())  13.6 us
    all_to_all x1, blocking collectives, body(): lax.all_to_all(q_blocks, ('dp', 'tensor'), 0, 0, axis_index_groups=PAIRED)  12.1 us
    all_to_all x1, starting transfers between devices, body(): blocks = lax.all_to_all(blocks.reshape(DP, HALF, COLS), 'dp', 0, 0)  10.5 us
    all_to_all x1, blocking collectives, body(): part = lax.all_to_all(part, 'dp', 0, 0, axis_index_groups=PLANE)  10.1 us
    ppermute x1, starting transfers between devices, body(): q_other = lax.ppermute(q_mine, 'dp', SWAP)  7.81 us
    all_to_all x1, blocking collectives, body(): near = lax.all_to_all(near, 'tensor', 0, 0, axis_index_groups=NEAR)  7.13 us
    ppermute x1, waiting for transfers between devices, body(): factor_t = lax.ppermute(q_start.T, ('dp', 'tensor'), factor_route())  5.74 us
  transfers between devices with their start and end apart: 4, of which 3 were waited for; matrix products, arithmetic and copies ran while one was open for 0% of the time, Pallas kernels for 0%

profile of v8, /device:TPU:1, one launch (start us, length us, event | category | flops | bytes accessed | tf_op | source)
XLA Modules:
  0.0 101.3 jit_solution(14429971789279247115)
XLA Ops:
  0.6 2.4 %shard_map.58 = bf16[16,2,64,256]{3,2,1,0:T(8,128)(2,1)} custom-call(bf16[1,128,4096]{2,1,0:T(8,128)(2,1)} %grad_ref.1, bf16[1,128,4096]{2,1,0:T(8,128)(2,1)} %error_ref.1), custom_call_target="tpu_custom_call" | custom-call | tf_op jit(solution)/shard_map/pallas_call | solution.py:253
  3.1 0.0 copy-start.2
  3.1 10.5 %all-to-all-start = ((bf16[32,64,256]{2,1,0:T(8,128)(2,1)}), bf16[32,64,256]{2,1,0:T(8,128)(2,1)S(1)}, u32[]{:S(2)}, u32[]{:S(2)}) async-start(bf16[32,64,256]{2,1,0:T(8,128)(2,1)} %bitcast.5), calls=%async_computation | async-start | bytes 2097152 | tf_op jit(solution)/shard_map/all_to_all | solution.py:267
  13.6 0.0 copy-done.2
  13.6 13.6 %collective-permute-start = (bf16[64,256]{1,0:T(8,128)(2,1)S(1)}, bf16[64,256]{1,0:T(8,128)(2,1)S(1)}, u32[]{:S(2)}, u32[]{:S(2)}) collective-permute-start(bf16[64,256]{1,0:T(8,128)(2,1)S(1)} %bitcast.7), channel_id=1, source_target_pairs={{0,8},{16,24},{32,7},{48,23},{96,9},{112,25},{128,6},{144,22},{384... | collective-permute-start | bytes 98312 | tf_op jit(solution)/shard_map/ppermute | solution.py:251
  27.2 5.7 %collective-permute-done.factor_ref = bf16[64,256]{1,0:T(8,128)(2,1)S(1)} collective-permute-done((bf16[64,256]{1,0:T(8,128)(2,1)S(1)}, bf16[64,256]{1,0:T(8,128)(2,1)S(1)}, u32[]{:S(2)}, u32[]{:S(2)}) %collective-permute-start) | collective-permute-done | bytes 32800 | tf_op jit(solution)/shard_map/ppermute | solution.py:251
  32.9 0.0 all-to-all-done.blocks_ref
  32.9 0.4 shard_map.59
  33.3 0.0 copy-start
  33.4 0.0 copy-start.1
  33.4 10.1 %all_to_all.20.share_ref = f32[16,32,128]{2,1,0:T(8,128)S(1)} all-to-all(f32[16,32,128]{2,1,0:T(8,128)S(1)} %get-tuple-element.14), channel_id=1, replica_groups={{0,32,64,96,128,160,192,224,256,288,320,352,384,416,448,480},{16,48,80,..., dimensions={0} | all-to-all | bytes 524288 | tf_op jit(solution)/shard_map/all_to_all | solution.py:271
  43.5 0.4 shard_map.60
  43.9 4.2 %collective-permute-start.1 = (f32[120,128]{1,0:T(8,128)S(1)}, f32[120,128]{1,0:T(8,128)S(1)}, u32[]{:S(2)}, u32[]{:S(2)}) collective-permute-start(f32[120,128]{1,0:T(8,128)S(1)} %get-tuple-element.17), channel_id=1, source_target_pairs={{0,16},{16,0},{32,48},{48,32},{64,80},{80,64},{96,112},{112,96},{1... | collective-permute-start | bytes 184328 | tf_op jit(solution)/shard_map/ppermute | solution.py:273
  48.1 0.9 collective-permute-done.1.got_ref
  49.0 0.1 shard_map.61
  49.1 7.1 %all_to_all.21.near_ref = f32[4,56,128]{2,1,0:T(8,128)S(1)} all-to-all(f32[4,56,128]{2,1,0:T(8,128)S(1)} %get-tuple-element.18), channel_id=1, replica_groups={{0,1,2,3},{4,5,6,7},{8,9,10,11},{12,13,14,15},{16,17,18,19},{20,21,22,2..., dimensions={0} | all-to-all | bytes 229376 | tf_op jit(solution)/shard_map/all_to_all | solution.py:275
  56.2 19.9 %all_gather.3.far_ref = f32[56,512]{1,0:T(8,128)S(1)} all-gather(f32[56,128]{1,0:T(8,128)S(1)} %shard_map.62), channel_id=1, replica_groups={{0,4,8,12},{1,5,9,13},{2,6,10,14},{3,7,11,15},{16,20,24,28},{17,21,25,2..., dimensions={1}, use_global_device_ids=true | all-gather | bytes 143360 | tf_op jit(solution)/shard_map/all_gather | solution.py:277
  76.2 2.4 %shard_map.63 = (bf16[32,32,128]{2,1,0:T(8,128)(2,1)S(1)}, bf16[128,64]{1,0:T(8,128)(2,1)S(1)}) custom-call(f32[56,512]{1,0:T(8,128)S(1)} %all_gather.3.far_ref, f32[128,64]{1,0:T(8,128)S(1)} %get-tuple-element.19.p_ref), custom_call_target="tpu_custom_call" | custom-call | tf_op jit(solution)/shard_map/pallas_call | solution.py:278
  78.5 12.1 %all_to_all.22.mine_ref = bf16[32,32,128]{2,1,0:T(8,128)(2,1)S(1)} all-to-all(bf16[32,32,128]{2,1,0:T(8,128)(2,1)S(1)} %get-tuple-element.20), channel_id=1, replica_groups={{0,32,64,96,128,160,192,224,256,288,320,352,384,416,448,480,1,33,65,97,..., dimensions={0} | all-to-all | bytes 524288 | tf_op jit(solution)/shard_map/all_to_all | solution.py:282
  90.7 7.8 %collective-permute-start.2 = (bf16[32,32,128]{2,1,0:T(8,128)(2,1)S(1)}, bf16[32,32,128]{2,1,0:T(8,128)(2,1)S(1)}, u32[]{:S(2)}, u32[]{:S(2)}) collective-permute-start(bf16[32,32,128]{2,1,0:T(8,128)(2,1)S(1)} %all_to_all.22.mine_ref), channel_id=1, source_target_pairs={{0,16},{16,0},{32,48},{48,32},{64,80},{80,64},{96,112},{112,96},{1... | collective-permute-start | bytes 786440 | tf_op jit(solution)/shard_map/ppermute | solution.py:283
  98.5 0.0 copy-done
  98.5 0.0 copy-done.1
  98.5 0.2 fusion.rows_ref
  98.7 0.9 collective-permute-done.2.other_ref
  99.6 1.7 %shard_map.64 = (bf16[128,4096]{1,0:T(8,128)(2,1)}, bf16[1,128,4096]{2,1,0:T(8,128)(2,1)}, f32[64,256]{1,0:T(8,128)}) custom-call(bf16[32,32,128]{2,1,0:T(8,128)(2,1)S(1)} %all_to_all.22.mine_ref, bf16[32,32,128]{2,1,0:T(8,128)(2,1)S(1)} %collective-permute-done.2.other_ref, bf16[128,64]{1,0:T(8,128)(2,1)S(1)} %get-tuple-element.21.p_ref, ...), custom_call_target="tpu_custom_call" | custom-call | tf_op jit(solution)/shard_map/pallas_call | solution.py:284
  (1 shorter events, 0.0 us)
Async XLA Ops:
  3.1 10.5 %copy-start.2 = (bf16[256,64]{0,1:T(8,128)(2,1)S(1)}, bf16[256,64]{0,1:T(8,128)(2,1)}, u32[]{:S(2)}) copy-start(bf16[256,64]{0,1:T(8,128)(2,1)} %param.5) | copy-start | bytes 98308
  3.1 29.8 %all-to-all-start = ((bf16[32,64,256]{2,1,0:T(8,128)(2,1)}), bf16[32,64,256]{2,1,0:T(8,128)(2,1)S(1)}, u32[]{:S(2)}, u32[]{:S(2)}) async-start(bf16[32,64,256]{2,1,0:T(8,128)(2,1)} %bitcast.5), calls=%async_computation | async-start | bytes 2097152 | tf_op jit(solution)/shard_map/all_to_all | solution.py:267
  13.6 19.3 %collective-permute-start = (bf16[64,256]{1,0:T(8,128)(2,1)S(1)}, bf16[64,256]{1,0:T(8,128)(2,1)S(1)}, u32[]{:S(2)}, u32[]{:S(2)}) collective-permute-start(bf16[64,256]{1,0:T(8,128)(2,1)S(1)} %bitcast.7), channel_id=1, source_target_pairs={{0,8},{16,24},{32,7},{48,23},{96,9},{112,25},{128,6},{144,22},{384... | collective-permute-start | bytes 98312 | tf_op jit(solution)/shard_map/ppermute | solution.py:251
  33.3 65.1 %copy-start = (bf16[1,128,4096]{2,1,0:T(8,128)(2,1)S(1)}, bf16[1,128,4096]{2,1,0:T(8,128)(2,1)}, u32[]{:S(2)}) copy-start(bf16[1,128,4096]{2,1,0:T(8,128)(2,1)} %grad_ref.1) | copy-start | bytes 3145732
  33.4 65.1 %copy-start.1 = (bf16[1,128,4096]{2,1,0:T(8,128)(2,1)S(1)}, bf16[1,128,4096]{2,1,0:T(8,128)(2,1)}, u32[]{:S(2)}) copy-start(bf16[1,128,4096]{2,1,0:T(8,128)(2,1)} %error_ref.1) | copy-start | bytes 3145732
  43.9 5.1 %collective-permute-start.1 = (f32[120,128]{1,0:T(8,128)S(1)}, f32[120,128]{1,0:T(8,128)S(1)}, u32[]{:S(2)}, u32[]{:S(2)}) collective-permute-start(f32[120,128]{1,0:T(8,128)S(1)} %get-tuple-element.17), channel_id=1, source_target_pairs={{0,16},{16,0},{32,48},{48,32},{64,80},{80,64},{96,112},{112,96},{1... | collective-permute-start | bytes 184328 | tf_op jit(solution)/shard_map/ppermute | solution.py:273
  90.7 9.0 %collective-permute-start.2 = (bf16[32,32,128]{2,1,0:T(8,128)(2,1)S(1)}, bf16[32,32,128]{2,1,0:T(8,128)(2,1)S(1)}, u32[]{:S(2)}, u32[]{:S(2)}) collective-permute-start(bf16[32,32,128]{2,1,0:T(8,128)(2,1)S(1)} %all_to_all.22.mine_ref), channel_id=1, source_target_pairs={{0,16},{16,0},{32,48},{48,32},{64,80},{80,64},{96,112},{112,96},{1... | collective-permute-start | bytes 786440 | tf_op jit(solution)/shard_map/ppermute | solution.py:283

commit v9 on v8

--- a/solution.py
+++ b/solution.py
@@ -178,7 +178,8 @@
             pivot, row = splat_row(cols[j][0], j), splat_row(strips[s], j)
             root = lax.rsqrt(pivot)
             done = jnp.where(sub == j, row * root, done)
-            factors = [c * (root * root) for c in cols[j]]
+            inverse = 1.0 / pivot
+            factors = [c * inverse for c in cols[j]]
             factors[0] = jnp.where(sub > j, factors[0], 0.0)
             for i in range(j + 1, 8):
                 entry = splat_row(cols[i][0], j)
@@ -212,11 +213,6 @@
         upper = jnp.concatenate([even[:, :R], odd[:, :R]], 1)
         lower = jnp.concatenate([even[:, R:], odd[:, R:]], 1)
         return jnp.concatenate([upper, lower], 0)
-
-    for c in range(CORES):
-        q_new_out[:, 128 * c : 128 * (c + 1)] = block(z, c).astype(F32)
-    q_copy = pltpu.make_async_copy(q_new_out, q_new_ref, q_sem)
-    q_copy.start()
 
     def copies(n):
         span = pl.ds(n * width, width)
@@ -234,6 +230,10 @@
             error_out[:, span] = (rows_ref[:, span].astype(F32) - full).astype(BF16)
         for copy in copies(n):
             copy.start()
+    for c in range(CORES):
+        q_new_out[:, 128 * c : 128 * (c + 1)] = block(z, c).astype(F32)
+    q_copy = pltpu.make_async_copy(q_new_out, q_new_ref, q_sem)
+    q_copy.start()
     for n in range(PARTS):
         for copy in copies(n):
             copy.wait()

time: 102 us -> 102 us (level)
  no operation moved by 1% of the time
where the time goes in v9:
time: 102 us; the launch traced here: 101 us
  blocking collectives  49.3 us (48%)
  starting transfers between devices  36.1 us (35%)
  waiting for transfers between devices  7.49 us (7%)
  Pallas kernels  7.43 us (7%)
    all_gather x1, blocking collectives, body(): lax.all_gather(far, 'tensor', axis_index_groups=FAR, axis=1, tiled=True)  19.9 us
    ppermute x1, starting transfers between devices, body(): factor_t = lax.ppermute(q_start.T, ('dp', 'tensor'), factor_route())  13.6 us
    all_to_all x1, blocking collectives, body(): lax.all_to_all(q_blocks, ('dp', 'tensor'), 0, 0, axis_index_groups=PAIRED)  12.1 us
    all_to_all x1, starting transfers between devices, body(): blocks = lax.all_to_all(blocks.reshape(DP, HALF, COLS), 'dp', 0, 0)  10.5 us
    all_to_all x1, blocking collectives, body(): part = lax.all_to_all(part, 'dp', 0, 0, axis_index_groups=PLANE)  10.1 us
    ppermute x1, starting transfers between devices, body(): q_other = lax.ppermute(q_mine, 'dp', SWAP)  7.81 us
    all_to_all x1, blocking collectives, body(): near = lax.all_to_all(near, 'tensor', 0, 0, axis_index_groups=NEAR)  7.13 us
    ppermute x1, waiting for transfers between devices, body(): factor_t = lax.ppermute(q_start.T, ('dp', 'tensor'), factor_route())  5.74 us
  transfers between devices with their start and end apart: 4, of which 3 were waited for; matrix products, arithmetic and copies ran while one was open for 0% of the time, Pallas kernels for 0%

profile of v9, /device:TPU:1, one launch (start us, length us, event | category | flops | bytes accessed | tf_op | source)
XLA Modules:
  0.0 101.3 jit_solution(4124812654894550183)
XLA Ops:
  0.6 2.4 %shard_map.58 = bf16[16,2,64,256]{3,2,1,0:T(8,128)(2,1)} custom-call(bf16[1,128,4096]{2,1,0:T(8,128)(2,1)} %grad_ref.1, bf16[1,128,4096]{2,1,0:T(8,128)(2,1)} %error_ref.1), custom_call_target="tpu_custom_call" | custom-call | tf_op jit(solution)/shard_map/pallas_call | solution.py:253
  3.1 0.0 copy-start.2
  3.1 10.5 %all-to-all-start = ((bf16[32,64,256]{2,1,0:T(8,128)(2,1)}), bf16[32,64,256]{2,1,0:T(8,128)(2,1)S(1)}, u32[]{:S(2)}, u32[]{:S(2)}) async-start(bf16[32,64,256]{2,1,0:T(8,128)(2,1)} %bitcast.5), calls=%async_computation | async-start | bytes 2097152 | tf_op jit(solution)/shard_map/all_to_all | solution.py:267
  13.6 0.0 copy-done.2
  13.6 13.6 %collective-permute-start = (bf16[64,256]{1,0:T(8,128)(2,1)S(1)}, bf16[64,256]{1,0:T(8,128)(2,1)S(1)}, u32[]{:S(2)}, u32[]{:S(2)}) collective-permute-start(bf16[64,256]{1,0:T(8,128)(2,1)S(1)} %bitcast.7), channel_id=1, source_target_pairs={{0,8},{16,24},{32,7},{48,23},{96,9},{112,25},{128,6},{144,22},{384... | collective-permute-start | bytes 98312 | tf_op jit(solution)/shard_map/ppermute | solution.py:251
  27.2 5.7 %collective-permute-done.factor_ref = bf16[64,256]{1,0:T(8,128)(2,1)S(1)} collective-permute-done((bf16[64,256]{1,0:T(8,128)(2,1)S(1)}, bf16[64,256]{1,0:T(8,128)(2,1)S(1)}, u32[]{:S(2)}, u32[]{:S(2)}) %collective-permute-start) | collective-permute-done | bytes 32800 | tf_op jit(solution)/shard_map/ppermute | solution.py:251
  32.9 0.0 all-to-all-done.blocks_ref
  32.9 0.4 shard_map.59
  33.3 0.0 copy-start
  33.4 0.0 copy-start.1
  33.4 10.1 %all_to_all.20.share_ref = f32[16,32,128]{2,1,0:T(8,128)S(1)} all-to-all(f32[16,32,128]{2,1,0:T(8,128)S(1)} %get-tuple-element.14), channel_id=1, replica_groups={{0,32,64,96,128,160,192,224,256,288,320,352,384,416,448,480},{16,48,80,..., dimensions={0} | all-to-all | bytes 524288 | tf_op jit(solution)/shard_map/all_to_all | solution.py:271
  43.5 0.4 shard_map.60
  43.9 4.2 %collective-permute-start.1 = (f32[120,128]{1,0:T(8,128)S(1)}, f32[120,128]{1,0:T(8,128)S(1)}, u32[]{:S(2)}, u32[]{:S(2)}) collective-permute-start(f32[120,128]{1,0:T(8,128)S(1)} %get-tuple-element.17), channel_id=1, source_target_pairs={{0,16},{16,0},{32,48},{48,32},{64,80},{80,64},{96,112},{112,96},{1... | collective-permute-start | bytes 184328 | tf_op jit(solution)/shard_map/ppermute | solution.py:273
  48.1 0.9 collective-permute-done.1.got_ref
  49.0 0.1 shard_map.61
  49.1 7.1 %all_to_all.21.near_ref = f32[4,56,128]{2,1,0:T(8,128)S(1)} all-to-all(f32[4,56,128]{2,1,0:T(8,128)S(1)} %get-tuple-element.18), channel_id=1, replica_groups={{0,1,2,3},{4,5,6,7},{8,9,10,11},{12,13,14,15},{16,17,18,19},{20,21,22,2..., dimensions={0} | all-to-all | bytes 229376 | tf_op jit(solution)/shard_map/all_to_all | solution.py:275
  56.2 19.9 %all_gather.3.far_ref = f32[56,512]{1,0:T(8,128)S(1)} all-gather(f32[56,128]{1,0:T(8,128)S(1)} %shard_map.62), channel_id=1, replica_groups={{0,4,8,12},{1,5,9,13},{2,6,10,14},{3,7,11,15},{16,20,24,28},{17,21,25,2..., dimensions={1}, use_global_device_ids=true | all-gather | bytes 143360 | tf_op jit(solution)/shard_map/all_gather | solution.py:277
  76.2 2.3 %shard_map.63 = (bf16[32,32,128]{2,1,0:T(8,128)(2,1)S(1)}, bf16[128,64]{1,0:T(8,128)(2,1)S(1)}) custom-call(f32[56,512]{1,0:T(8,128)S(1)} %all_gather.3.far_ref, f32[128,64]{1,0:T(8,128)S(1)} %get-tuple-element.19.p_ref), custom_call_target="tpu_custom_call" | custom-call | tf_op jit(solution)/shard_map/pallas_call | solution.py:278
  78.5 12.1 %all_to_all.22.mine_ref = bf16[32,32,128]{2,1,0:T(8,128)(2,1)S(1)} all-to-all(bf16[32,32,128]{2,1,0:T(8,128)(2,1)S(1)} %get-tuple-element.20), channel_id=1, replica_groups={{0,32,64,96,128,160,192,224,256,288,320,352,384,416,448,480,1,33,65,97,..., dimensions={0} | all-to-all | bytes 524288 | tf_op jit(solution)/shard_map/all_to_all | solution.py:282
  90.6 7.8 %collective-permute-start.2 = (bf16[32,32,128]{2,1,0:T(8,128)(2,1)S(1)}, bf16[32,32,128]{2,1,0:T(8,128)(2,1)S(1)}, u32[]{:S(2)}, u32[]{:S(2)}) collective-permute-start(bf16[32,32,128]{2,1,0:T(8,128)(2,1)S(1)} %all_to_all.22.mine_ref), channel_id=1, source_target_pairs={{0,16},{16,0},{32,48},{48,32},{64,80},{80,64},{96,112},{112,96},{1... | collective-permute-start | bytes 786440 | tf_op jit(solution)/shard_map/ppermute | solution.py:283
  98.4 0.0 copy-done
  98.5 0.0 copy-done.1
  98.5 0.2 fusion.rows_ref
  98.7 0.9 collective-permute-done.2.other_ref
  99.6 1.7 %shard_map.64 = (bf16[128,4096]{1,0:T(8,128)(2,1)}, bf16[1,128,4096]{2,1,0:T(8,128)(2,1)}, f32[64,256]{1,0:T(8,128)}) custom-call(bf16[32,32,128]{2,1,0:T(8,128)(2,1)S(1)} %all_to_all.22.mine_ref, bf16[32,32,128]{2,1,0:T(8,128)(2,1)S(1)} %collective-permute-done.2.other_ref, bf16[128,64]{1,0:T(8,128)(2,1)S(1)} %get-tuple-element.21.p_ref, ...), custom_call_target="tpu_custom_call" | custom-call | tf_op jit(solution)/shard_map/pallas_call | solution.py:284
  (1 shorter events, 0.0 us)
Async XLA Ops:
  3.1 10.5 %copy-start.2 = (bf16[256,64]{0,1:T(8,128)(2,1)S(1)}, bf16[256,64]{0,1:T(8,128)(2,1)}, u32[]{:S(2)}) copy-start(bf16[256,64]{0,1:T(8,128)(2,1)} %param.5) | copy-start | bytes 98308
  3.1 29.8 %all-to-all-start = ((bf16[32,64,256]{2,1,0:T(8,128)(2,1)}), bf16[32,64,256]{2,1,0:T(8,128)(2,1)S(1)}, u32[]{:S(2)}, u32[]{:S(2)}) async-start(bf16[32,64,256]{2,1,0:T(8,128)(2,1)} %bitcast.5), calls=%async_computation | async-start | bytes 2097152 | tf_op jit(solution)/shard_map/all_to_all | solution.py:267
  13.6 19.3 %collective-permute-start = (bf16[64,256]{1,0:T(8,128)(2,1)S(1)}, bf16[64,256]{1,0:T(8,128)(2,1)S(1)}, u32[]{:S(2)}, u32[]{:S(2)}) collective-permute-start(bf16[64,256]{1,0:T(8,128)(2,1)S(1)} %bitcast.7), channel_id=1, source_target_pairs={{0,8},{16,24},{32,7},{48,23},{96,9},{112,25},{128,6},{144,22},{384... | collective-permute-start | bytes 98312 | tf_op jit(solution)/shard_map/ppermute | solution.py:251
  33.3 65.1 %copy-start = (bf16[1,128,4096]{2,1,0:T(8,128)(2,1)S(1)}, bf16[1,128,4096]{2,1,0:T(8,128)(2,1)}, u32[]{:S(2)}) copy-start(bf16[1,128,4096]{2,1,0:T(8,128)(2,1)} %grad_ref.1) | copy-start | bytes 3145732
  33.4 65.1 %copy-start.1 = (bf16[1,128,4096]{2,1,0:T(8,128)(2,1)S(1)}, bf16[1,128,4096]{2,1,0:T(8,128)(2,1)}, u32[]{:S(2)}) copy-start(bf16[1,128,4096]{2,1,0:T(8,128)(2,1)} %error_ref.1) | copy-start | bytes 3145732
  43.9 5.1 %collective-permute-start.1 = (f32[120,128]{1,0:T(8,128)S(1)}, f32[120,128]{1,0:T(8,128)S(1)}, u32[]{:S(2)}, u32[]{:S(2)}) collective-permute-start(f32[120,128]{1,0:T(8,128)S(1)} %get-tuple-element.17), channel_id=1, source_target_pairs={{0,16},{16,0},{32,48},{48,32},{64,80},{80,64},{96,112},{112,96},{1... | collective-permute-start | bytes 184328 | tf_op jit(solution)/shard_map/ppermute | solution.py:273
  90.6 9.0 %collective-permute-start.2 = (bf16[32,32,128]{2,1,0:T(8,128)(2,1)S(1)}, bf16[32,32,128]{2,1,0:T(8,128)(2,1)S(1)}, u32[]{:S(2)}, u32[]{:S(2)}) collective-permute-start(bf16[32,32,128]{2,1,0:T(8,128)(2,1)S(1)} %all_to_all.22.mine_ref), channel_id=1, source_target_pairs={{0,16},{16,0},{32,48},{48,32},{64,80},{80,64},{96,112},{112,96},{1... | collective-permute-start | bytes 786440 | tf_op jit(solution)/shard_map/ppermute | solution.py:283

commit v10 on v8

--- a/solution.py
+++ b/solution.py
@@ -16,6 +16,7 @@
 COLS = D // CHIPS
 R = 64
 GRAM = 24
+WRITES = 8
 PARTS = 4
 HIGH = lax.Precision.HIGHEST
 F32, BF16 = jnp.float32, jnp.bfloat16
@@ -200,7 +201,7 @@
 def update_kernel(
     mine_ref, other_ref, p_ref, rows_ref, update_ref, error_ref, q_new_ref, update_out, error_out, q_new_out, sems, q_sem
 ):
-    width = D // PARTS
+    width = D // WRITES
     z = lax.axis_index("tensor")
     first = lax.rem(lax.axis_index("dp"), CORES) == 0
 
@@ -225,7 +226,7 @@
             pltpu.make_async_copy(error_out.at[:, span], error_ref.at[0, :, span], sems.at[1, n]),
         ]
 
-    for n in range(PARTS):
+    for n in range(WRITES):
         for k in range(n * width // COLS, (n + 1) * width // COLS):
             q = jnp.concatenate([block(k, c) for c in range(CORES)], 1)
             full = dot(p_ref[...], q, ((1,), (0,)))
@@ -234,7 +235,7 @@
             error_out[:, span] = (rows_ref[:, span].astype(F32) - full).astype(BF16)
         for copy in copies(n):
             copy.start()
-    for n in range(PARTS):
+    for n in range(WRITES):
         for copy in copies(n):
             copy.wait()
     q_copy.wait()
@@ -290,7 +291,7 @@
             pltpu.VMEM((ROWS, D), BF16),
             pltpu.VMEM((ROWS, D), BF16),
             pltpu.VMEM((R, COLS), F32),
-            pltpu.SemaphoreType.DMA((2, PARTS)),
+            pltpu.SemaphoreType.DMA((2, WRITES)),
             pltpu.SemaphoreType.DMA,
         ],
     )(q_mine, q_other, p_round, corrected)

time: 102 us -> 102 us (level)
  no operation moved by 1% of the time
where the time goes in v10:
time: 102 us; the launch traced here: 101 us
  blocking collectives  49.3 us (48%)
  starting transfers between devices  36.1 us (35%)
  waiting for transfers between devices  7.49 us (7%)
  Pallas kernels  7.48 us (7%)
    all_gather x1, blocking collectives, body(): lax.all_gather(far, 'tensor', axis_index_groups=FAR, axis=1, tiled=True)  19.9 us
    ppermute x1, starting transfers between devices, body(): factor_t = lax.ppermute(q_start.T, ('dp', 'tensor'), factor_route())  13.6 us
    all_to_all x1, blocking collectives, body(): lax.all_to_all(q_blocks, ('dp', 'tensor'), 0, 0, axis_index_groups=PAIRED)  12.1 us
    all_to_all x1, starting transfers between devices, body(): blocks = lax.all_to_all(blocks.reshape(DP, HALF, COLS), 'dp', 0, 0)  10.5 us
    all_to_all x1, blocking collectives, body(): part = lax.all_to_all(part, 'dp', 0, 0, axis_index_groups=PLANE)  10.1 us
    ppermute x1, starting transfers between devices, body(): q_other = lax.ppermute(q_mine, 'dp', SWAP)  7.81 us
    all_to_all x1, blocking collectives, body(): near = lax.all_to_all(near, 'tensor', 0, 0, axis_index_groups=NEAR)  7.13 us
    ppermute x1, waiting for transfers between devices, body(): factor_t = lax.ppermute(q_start.T, ('dp', 'tensor'), factor_route())  5.74 us
  transfers between devices with their start and end apart: 4, of which 3 were waited for; matrix products, arithmetic and copies ran while one was open for 0% of the time, Pallas kernels for 0%

profile of v10, /device:TPU:1, one launch (start us, length us, event | category | flops | bytes accessed | tf_op | source)
XLA Modules:
  0.0 101.3 jit_solution(10339674544097878984)
XLA Ops:
  0.6 2.4 %shard_map.58 = bf16[16,2,64,256]{3,2,1,0:T(8,128)(2,1)} custom-call(bf16[1,128,4096]{2,1,0:T(8,128)(2,1)} %grad_ref.1, bf16[1,128,4096]{2,1,0:T(8,128)(2,1)} %error_ref.1), custom_call_target="tpu_custom_call" | custom-call | tf_op jit(solution)/shard_map/pallas_call | solution.py:254
  3.1 0.0 copy-start.2
  3.1 10.5 %all-to-all-start = ((bf16[32,64,256]{2,1,0:T(8,128)(2,1)}), bf16[32,64,256]{2,1,0:T(8,128)(2,1)S(1)}, u32[]{:S(2)}, u32[]{:S(2)}) async-start(bf16[32,64,256]{2,1,0:T(8,128)(2,1)} %bitcast.5), calls=%async_computation | async-start | bytes 2097152 | tf_op jit(solution)/shard_map/all_to_all | solution.py:268
  13.6 0.0 copy-done.2
  13.6 13.6 %collective-permute-start = (bf16[64,256]{1,0:T(8,128)(2,1)S(1)}, bf16[64,256]{1,0:T(8,128)(2,1)S(1)}, u32[]{:S(2)}, u32[]{:S(2)}) collective-permute-start(bf16[64,256]{1,0:T(8,128)(2,1)S(1)} %bitcast.7), channel_id=1, source_target_pairs={{0,8},{16,24},{32,7},{48,23},{96,9},{112,25},{128,6},{144,22},{384... | collective-permute-start | bytes 98312 | tf_op jit(solution)/shard_map/ppermute | solution.py:252
  27.2 5.7 %collective-permute-done.factor_ref = bf16[64,256]{1,0:T(8,128)(2,1)S(1)} collective-permute-done((bf16[64,256]{1,0:T(8,128)(2,1)S(1)}, bf16[64,256]{1,0:T(8,128)(2,1)S(1)}, u32[]{:S(2)}, u32[]{:S(2)}) %collective-permute-start) | collective-permute-done | bytes 32800 | tf_op jit(solution)/shard_map/ppermute | solution.py:252
  32.9 0.0 all-to-all-done.blocks_ref
  32.9 0.4 shard_map.59
  33.3 0.0 copy-start
  33.4 0.0 copy-start.1
  33.4 10.1 %all_to_all.20.share_ref = f32[16,32,128]{2,1,0:T(8,128)S(1)} all-to-all(f32[16,32,128]{2,1,0:T(8,128)S(1)} %get-tuple-element.14), channel_id=1, replica_groups={{0,32,64,96,128,160,192,224,256,288,320,352,384,416,448,480},{16,48,80,..., dimensions={0} | all-to-all | bytes 524288 | tf_op jit(solution)/shard_map/all_to_all | solution.py:272
  43.5 0.4 shard_map.60
  43.9 4.2 %collective-permute-start.1 = (f32[120,128]{1,0:T(8,128)S(1)}, f32[120,128]{1,0:T(8,128)S(1)}, u32[]{:S(2)}, u32[]{:S(2)}) collective-permute-start(f32[120,128]{1,0:T(8,128)S(1)} %get-tuple-element.17), channel_id=1, source_target_pairs={{0,16},{16,0},{32,48},{48,32},{64,80},{80,64},{96,112},{112,96},{1... | collective-permute-start | bytes 184328 | tf_op jit(solution)/shard_map/ppermute | solution.py:274
  48.1 0.9 collective-permute-done.1.got_ref
  49.0 0.1 shard_map.61
  49.1 7.1 %all_to_all.21.near_ref = f32[4,56,128]{2,1,0:T(8,128)S(1)} all-to-all(f32[4,56,128]{2,1,0:T(8,128)S(1)} %get-tuple-element.18), channel_id=1, replica_groups={{0,1,2,3},{4,5,6,7},{8,9,10,11},{12,13,14,15},{16,17,18,19},{20,21,22,2..., dimensions={0} | all-to-all | bytes 229376 | tf_op jit(solution)/shard_map/all_to_all | solution.py:276
  56.2 19.9 %all_gather.3.far_ref = f32[56,512]{1,0:T(8,128)S(1)} all-gather(f32[56,128]{1,0:T(8,128)S(1)} %shard_map.62), channel_id=1, replica_groups={{0,4,8,12},{1,5,9,13},{2,6,10,14},{3,7,11,15},{16,20,24,28},{17,21,25,2..., dimensions={1}, use_global_device_ids=true | all-gather | bytes 143360 | tf_op jit(solution)/shard_map/all_gather | solution.py:278
  76.2 2.4 %shard_map.63 = (bf16[32,32,128]{2,1,0:T(8,128)(2,1)S(1)}, bf16[128,64]{1,0:T(8,128)(2,1)S(1)}) custom-call(f32[56,512]{1,0:T(8,128)S(1)} %all_gather.3.far_ref, f32[128,64]{1,0:T(8,128)S(1)} %get-tuple-element.19.p_ref), custom_call_target="tpu_custom_call" | custom-call | tf_op jit(solution)/shard_map/pallas_call | solution.py:279
  78.5 12.1 %all_to_all.22.mine_ref = bf16[32,32,128]{2,1,0:T(8,128)(2,1)S(1)} all-to-all(bf16[32,32,128]{2,1,0:T(8,128)(2,1)S(1)} %get-tuple-element.20), channel_id=1, replica_groups={{0,32,64,96,128,160,192,224,256,288,320,352,384,416,448,480,1,33,65,97,..., dimensions={0} | all-to-all | bytes 524288 | tf_op jit(solution)/shard_map/all_to_all | solution.py:283
  90.7 7.8 %collective-permute-start.2 = (bf16[32,32,128]{2,1,0:T(8,128)(2,1)S(1)}, bf16[32,32,128]{2,1,0:T(8,128)(2,1)S(1)}, u32[]{:S(2)}, u32[]{:S(2)}) collective-permute-start(bf16[32,32,128]{2,1,0:T(8,128)(2,1)S(1)} %all_to_all.22.mine_ref), channel_id=1, source_target_pairs={{0,16},{16,0},{32,48},{48,32},{64,80},{80,64},{96,112},{112,96},{1... | collective-permute-start | bytes 786440 | tf_op jit(solution)/shard_map/ppermute | solution.py:284
  98.5 0.0 copy-done
  98.5 0.0 copy-done.1
  98.5 0.2 fusion.rows_ref
  98.7 0.9 collective-permute-done.2.other_ref
  99.6 1.7 %shard_map.64 = (bf16[128,4096]{1,0:T(8,128)(2,1)}, bf16[1,128,4096]{2,1,0:T(8,128)(2,1)}, f32[64,256]{1,0:T(8,128)}) custom-call(bf16[32,32,128]{2,1,0:T(8,128)(2,1)S(1)} %all_to_all.22.mine_ref, bf16[32,32,128]{2,1,0:T(8,128)(2,1)S(1)} %collective-permute-done.2.other_ref, bf16[128,64]{1,0:T(8,128)(2,1)S(1)} %get-tuple-element.21.p_ref, ...), custom_call_target="tpu_custom_call" | custom-call | tf_op jit(solution)/shard_map/pallas_call | solution.py:285
  (1 shorter events, 0.0 us)
Async XLA Ops:
  3.1 10.5 %copy-start.2 = (bf16[256,64]{0,1:T(8,128)(2,1)S(1)}, bf16[256,64]{0,1:T(8,128)(2,1)}, u32[]{:S(2)}) copy-start(bf16[256,64]{0,1:T(8,128)(2,1)} %param.5) | copy-start | bytes 98308
  3.1 29.8 %all-to-all-start = ((bf16[32,64,256]{2,1,0:T(8,128)(2,1)}), bf16[32,64,256]{2,1,0:T(8,128)(2,1)S(1)}, u32[]{:S(2)}, u32[]{:S(2)}) async-start(bf16[32,64,256]{2,1,0:T(8,128)(2,1)} %bitcast.5), calls=%async_computation | async-start | bytes 2097152 | tf_op jit(solution)/shard_map/all_to_all | solution.py:268
  13.6 19.3 %collective-permute-start = (bf16[64,256]{1,0:T(8,128)(2,1)S(1)}, bf16[64,256]{1,0:T(8,128)(2,1)S(1)}, u32[]{:S(2)}, u32[]{:S(2)}) collective-permute-start(bf16[64,256]{1,0:T(8,128)(2,1)S(1)} %bitcast.7), channel_id=1, source_target_pairs={{0,8},{16,24},{32,7},{48,23},{96,9},{112,25},{128,6},{144,22},{384... | collective-permute-start | bytes 98312 | tf_op jit(solution)/shard_map/ppermute | solution.py:252
  33.3 65.1 %copy-start = (bf16[1,128,4096]{2,1,0:T(8,128)(2,1)S(1)}, bf16[1,128,4096]{2,1,0:T(8,128)(2,1)}, u32[]{:S(2)}) copy-start(bf16[1,128,4096]{2,1,0:T(8,128)(2,1)} %grad_ref.1) | copy-start | bytes 3145732
  33.4 65.1 %copy-start.1 = (bf16[1,128,4096]{2,1,0:T(8,128)(2,1)S(1)}, bf16[1,128,4096]{2,1,0:T(8,128)(2,1)}, u32[]{:S(2)}) copy-start(bf16[1,128,4096]{2,1,0:T(8,128)(2,1)} %error_ref.1) | copy-start | bytes 3145732
  43.9 5.1 %collective-permute-start.1 = (f32[120,128]{1,0:T(8,128)S(1)}, f32[120,128]{1,0:T(8,128)S(1)}, u32[]{:S(2)}, u32[]{:S(2)}) collective-permute-start(f32[120,128]{1,0:T(8,128)S(1)} %get-tuple-element.17), channel_id=1, source_target_pairs={{0,16},{16,0},{32,48},{48,32},{64,80},{80,64},{96,112},{112,96},{1... | collective-permute-start | bytes 184328 | tf_op jit(solution)/shard_map/ppermute | solution.py:274
  90.7 9.0 %collective-permute-start.2 = (bf16[32,32,128]{2,1,0:T(8,128)(2,1)S(1)}, bf16[32,32,128]{2,1,0:T(8,128)(2,1)S(1)}, u32[]{:S(2)}, u32[]{:S(2)}) collective-permute-start(bf16[32,32,128]{2,1,0:T(8,128)(2,1)S(1)} %all_to_all.22.mine_ref), channel_id=1, source_target_pairs={{0,16},{16,0},{32,48},{48,32},{64,80},{80,64},{96,112},{112,96},{1... | collective-permute-start | bytes 786440 | tf_op jit(solution)/shard_map/ppermute | solution.py:284
